TPU v7x, 512 devices: a whole 4x8x8 slice. The times are simulated.
512 devices in a mesh: dp: 4 (over z_lo, core), ctx: 32 (over y, z_hi), tp: 4 (over x).
Axes of the slice: x: 4, y: 8, z: 8 (z_hi: 4, z_lo: 2; z = z_hi * 2 + z_lo), core: 2. Of those that a mesh axis runs over, the one named last changes fastest.
Arguments:
- queries_raw: bfloat16 [4, 8192, 4096], P('dp', 'ctx', 'tp'), may hold values from -400 to 400
- keys_raw: bfloat16 [4, 8192, 512], P('dp', 'ctx', 'tp'), may hold values from -400 to 400
- values: bfloat16 [4, 8192, 512], P('dp', 'ctx', 'tp'), may hold values from -6 to 6
- grad_out: bfloat16 [4, 8192, 4096], P('dp', 'ctx', 'tp'), may hold values from -6 to 6
- q_gain: float32 [128], replicated, may hold values from 0.5 to 8
- k_gain: float32 [128], replicated, may hold values from 0.5 to 8
- doc_lengths: int32 [4, 64], P('dp'), may hold values from 1 to 1024, 8192 in all within a row
Outputs:
- queries_grad: bfloat16 [4, 8192, 4096], P('dp', 'ctx', 'tp')
- keys_grad: bfloat16 [4, 8192, 512], P('dp', 'ctx', 'tp')
- values_grad: bfloat16 [4, 8192, 512], P('dp', 'ctx', 'tp')
- gain_grads: float32 [2, 128], replicated
Inputs may be any that keep to these rules, and one draw needn't show every extreme that they name: `doc_lengths`: each pack's documents lie end to end and fill its 8192 tokens.
All inputs are finite; a program needn't handle non-finite values.
Results may differ from a plain program's by a relative error of at most 0.024.
The roundings to bfloat16 on the way count: a program that leaves them out, or rounds other values in their place, can miss the bound.
Values may be sent and summed in bfloat16 or wider, within the bound.
No kernel may reach another device: no remote copies, remote signals or barrier semaphores. Data moves between devices by JAX's collectives and lax.ppermute only.
A program may use at most 64 MiB of HBM per device.

v0:
```python
import math

import jax
import jax.numpy as jnp
from jax import lax
from jax.sharding import PartitionSpec as P

REACH = 4


EPSILON = 1e-06
ROPE_BASE = 1000000.0


def shifted(block, axis, distance):
    devices = range(lax.axis_size(axis))
    route = [(i - distance, i) for i in devices if i - distance in devices]
    return lax.ppermute(block, axis, route)


def locate(tok_index, starts):
    within = starts[None, :] <= tok_index[:, None]
    doc_id = jnp.sum(within.astype(jnp.int32), axis=1) - 1
    doc_start = jnp.max(jnp.where(within, starts[None, :], 0), axis=1)
    return (doc_id, tok_index - doc_start)


def rotation(position, head_width):
    half_width = head_width // 2
    inv_freq = jnp.exp(
        jnp.arange(half_width, dtype=jnp.float32) * (-2.0 * math.log(ROPE_BASE) / head_width)
    )
    angles = position.astype(jnp.float32)[:, None] * inv_freq[None, :]
    return (jnp.cos(angles)[:, None, :], jnp.sin(angles)[:, None, :])


def norm_rope(source, gain_vec, cos_part, sine_part):
    values32 = source.astype(jnp.float32)
    inv_rms = lax.rsqrt(jnp.mean(values32 * values32, axis=-1, keepdims=True) + EPSILON)
    normed = values32 * inv_rms
    scaled = normed * gain_vec
    half_width = scaled.shape[-1] // 2
    lower = scaled[..., :half_width]
    upper = scaled[..., half_width:]
    rotated = jnp.concatenate(
        [lower * cos_part - upper * sine_part, upper * cos_part + lower * sine_part], axis=-1
    )
    return (rotated, normed, inv_rms)


def unrope_norm(rot_grad, gain_vec, normed, inv_rms, cos_part, sine_part):
    half_width = rot_grad.shape[-1] // 2
    grad_lower = rot_grad[..., :half_width]
    grad_upper = rot_grad[..., half_width:]
    norm_grad = jnp.concatenate(
        [
            grad_lower * cos_part + grad_upper * sine_part,
            grad_upper * cos_part - grad_lower * sine_part,
        ],
        axis=-1,
    )
    gain_term = jnp.sum(norm_grad * normed, axis=(0, 1))
    gained = norm_grad * gain_vec
    raw_grad = (gained - normed * jnp.mean(gained * normed, axis=-1, keepdims=True)) * inv_rms
    return (raw_grad, gain_term)


def attend(q_rot, grad_rows, window_keys, window_values, allowed):
    tok_rows, q_heads, head_width = q_rot.shape
    key_count, kv_heads, _ = window_keys.shape
    group_size = q_heads // kv_heads
    unit_count = q_heads // 2
    score_scale = head_width ** (-0.5)

    def by_units(tensor):
        return (
            tensor.reshape(tok_rows, unit_count, 2, head_width)
            .transpose(1, 2, 0, 3)
            .reshape(unit_count, 2 * tok_rows, head_width)
        )

    unit_keys = jnp.repeat(window_keys.transpose(1, 0, 2), group_size // 2, axis=0)
    unit_values = jnp.repeat(window_values.transpose(1, 0, 2), group_size // 2, axis=0)

    def one_unit(operands):
        queries, gradient, keyset, valueset = operands
        scores = (
            jnp.dot(queries, keyset.T, preferred_element_type=jnp.float32).reshape(
                2, tok_rows, key_count
            )
            * score_scale
        )
        scores = jnp.where(allowed[None], scores, -1e30)
        row_max = jnp.max(scores, axis=-1, keepdims=True)
        row_sum = jnp.sum(jnp.exp(scores - row_max), axis=-1, keepdims=True)
        weights = jnp.exp(scores - (row_max + jnp.log(row_sum)))
        weights_b = weights.astype(jnp.bfloat16).reshape(2 * tok_rows, key_count)
        attn_out = jnp.dot(weights_b, valueset, preferred_element_type=jnp.float32)
        row_delta = jnp.sum(gradient.astype(jnp.float32) * attn_out, axis=-1).reshape(
            2, tok_rows, 1
        )
        weight_grad = jnp.dot(gradient, valueset.T, preferred_element_type=jnp.float32).reshape(
            2, tok_rows, key_count
        )
        score_grad = (
            (weights * (weight_grad - row_delta) * score_scale)
            .astype(jnp.bfloat16)
            .reshape(2 * tok_rows, key_count)
        )
        q_grad = jnp.dot(score_grad, keyset, preferred_element_type=jnp.float32)
        k_grad = jnp.dot(score_grad.T, queries, preferred_element_type=jnp.float32)
        v_grad = jnp.dot(weights_b.T, gradient, preferred_element_type=jnp.float32)
        return (q_grad, k_grad, v_grad)

    q_grad, k_grad, v_grad = lax.map(
        one_unit, (by_units(q_rot), by_units(grad_rows), unit_keys, unit_values)
    )
    q_grad = (
        q_grad.reshape(unit_count, 2, tok_rows, head_width)
        .transpose(2, 0, 1, 3)
        .reshape(tok_rows, q_heads, head_width)
    )
    k_grad = (
        k_grad.reshape(kv_heads, group_size // 2, key_count, head_width)
        .sum(axis=1)
        .transpose(1, 0, 2)
    )
    v_grad = (
        v_grad.reshape(kv_heads, group_size // 2, key_count, head_width)
        .sum(axis=1)
        .transpose(1, 0, 2)
    )
    return (q_grad, k_grad, v_grad)


def on_device(queries_raw, keys_raw, values, grad_out, q_gain, k_gain, doc_lengths):
    tok_rows = queries_raw.shape[1]
    head_width = q_gain.shape[0]
    q_heads = queries_raw.shape[2] // head_width
    kv_heads = keys_raw.shape[2] // head_width
    ctx_count = lax.axis_size("ctx")
    reach_back = min(REACH, ctx_count - 1)
    window_len = (reach_back + 1) * tok_rows
    shard_index = lax.axis_index("ctx")
    lengths = doc_lengths[0]
    starts = jnp.cumsum(lengths) - lengths
    tok_index = shard_index * tok_rows + jnp.arange(tok_rows, dtype=jnp.int32)
    doc_q, position = locate(tok_index, starts)
    cos_part, sine_part = rotation(position, head_width)
    q_rot, q_normed, q_inv = norm_rope(
        queries_raw[0].reshape(tok_rows, q_heads, head_width), q_gain, cos_part, sine_part
    )
    k_rot, k_normed, k_inv = norm_rope(
        keys_raw[0].reshape(tok_rows, kv_heads, head_width), k_gain, cos_part, sine_part
    )
    q_bf = q_rot.astype(jnp.bfloat16)
    own_block = jnp.stack(
        [k_rot.astype(jnp.bfloat16).reshape(tok_rows, kv_heads * head_width), values[0]]
    )
    received = [own_block]
    current = own_block
    for distance in range(reach_back):
        current = shifted(current, "ctx", 1)
        received.append(current)
    window = jnp.concatenate(received[::-1], axis=1)
    window_keys = window[0].reshape(window_len, kv_heads, head_width)
    window_values = window[1].reshape(window_len, kv_heads, head_width)
    key_index = (shard_index - reach_back) * tok_rows + jnp.arange(window_len, dtype=jnp.int32)
    doc_k, _ = locate(key_index, starts)
    allowed = (doc_k[None, :] == doc_q[:, None]) & (key_index[None, :] <= tok_index[:, None])
    grad_rows = grad_out[0].reshape(tok_rows, q_heads, head_width)
    q_rot_grad, k_win_grad, v_win_grad = attend(
        q_bf, grad_rows, window_keys, window_values, allowed
    )
    pieces = jnp.stack(
        [
            k_win_grad.reshape(window_len, kv_heads * head_width),
            v_win_grad.reshape(window_len, kv_heads * head_width),
        ]
    )
    pieces = pieces.reshape(2, reach_back + 1, tok_rows, kv_heads * head_width)
    summed = pieces[:, 0]
    for distance in range(1, reach_back + 1):
        summed = (
            shifted(summed.astype(jnp.bfloat16), "ctx", -1).astype(summed.dtype)
            + pieces[:, distance]
        )
    k_rot_grad = summed[0].reshape(tok_rows, kv_heads, head_width)
    q_raw_grad, q_term = unrope_norm(q_rot_grad, q_gain, q_normed, q_inv, cos_part, sine_part)
    k_raw_grad, k_term = unrope_norm(k_rot_grad, k_gain, k_normed, k_inv, cos_part, sine_part)
    loss_scale = (lax.axis_size("dp") * ctx_count * tok_rows) ** (-0.5)
    gain_grads = lax.psum(jnp.stack([q_term, k_term]), ("dp", "ctx", "tp")) * loss_scale
    queries_grad = q_raw_grad.astype(jnp.bfloat16).reshape(1, tok_rows, q_heads * head_width)
    keys_grad = k_raw_grad.astype(jnp.bfloat16).reshape(1, tok_rows, kv_heads * head_width)
    values_grad = summed[1].astype(jnp.bfloat16).reshape(1, tok_rows, kv_heads * head_width)
    return (queries_grad, keys_grad, values_grad, gain_grads)


def solution(mesh):
    return jax.shard_map(
        on_device,
        mesh=mesh,
        in_specs=(
            P("dp", "ctx", "tp"),
            P("dp", "ctx", "tp"),
            P("dp", "ctx", "tp"),
            P("dp", "ctx", "tp"),
            P(),
            P(),
            P("dp", None),
        ),
        out_specs=(P("dp", "ctx", "tp"), P("dp", "ctx", "tp"), P("dp", "ctx", "tp"), P()),
        check_vma=False,
    )
```

profile of v0, /device:TPU:1, one launch (start us, length us, event | category | flops | bytes accessed | tf_op | source)
XLA Modules:
  0.0 273.9 jit_solution(16740765118436817215)
XLA Ops:
  0.7 0.9 reduce-window_clone.1
  2.2 0.9 fusion.56
  3.3 0.9 fusion.53
  4.9 1.0 pad_maximum_fusion.3
  5.9 6.6 %collective-permute-start = (bf16[2,256,128]{2,1,0:T(8,128)(2,1)S(1)}, bf16[2,256,128]{2,1,0:T(8,128)(2,1)S(1)}, u32[]{:S(2)}, u32[]{:S(2)}) collective-permute-start(bf16[2,256,128]{2,1,0:T(8,128)(2,1)S(1)} %pad_maximum_fusion.3), channel_id=1, source_target_pairs={{0,4},{4,8},{8,12},{12,16},{16,20},{20,24},{24,28},{28,32},{32,36}... | collective-permute-start | bytes 393224 | tf_op jit(solution)/shard_map/ppermute | solution.py:18
  13.1 1.2 convert_bitcast_fusion
  16.4 8.7 %collective-permute-start.1 = (bf16[2,256,128]{2,1,0:T(8,128)(2,1)S(1)}, bf16[2,256,128]{2,1,0:T(8,128)(2,1)S(1)}, u32[]{:S(2)}, u32[]{:S(2)}) collective-permute-start(bf16[2,256,128]{2,1,0:T(8,128)(2,1)S(1)} %collective-permute-done), channel_id=1, source_target_pairs={{0,4},{4,8},{8,12},{12,16},{16,20},{20,24},{24,28},{28,32},{32,36}... | collective-permute-start | bytes 393224 | tf_op jit(solution)/shard_map/ppermute | solution.py:18
  25.3 2.1 collective-permute-done.1
  27.4 9.7 %collective-permute-start.2 = (bf16[2,256,128]{2,1,0:T(8,128)(2,1)S(1)}, bf16[2,256,128]{2,1,0:T(8,128)(2,1)}, u32[]{:S(2)}, u32[]{:S(2)}) collective-permute-start(bf16[2,256,128]{2,1,0:T(8,128)(2,1)S(1)} %collective-permute-done.1), channel_id=1, source_target_pairs={{0,4},{4,8},{8,12},{12,16},{16,20},{20,24},{24,28},{28,32},{32,36}... | collective-permute-start | bytes 393224 | tf_op jit(solution)/shard_map/ppermute | solution.py:18
  37.2 1.3 collective-permute-done.2
  38.4 8.2 %collective-permute-start.3 = (bf16[2,256,128]{2,1,0:T(8,128)(2,1)}, bf16[2,256,128]{2,1,0:T(8,128)(2,1)}, u32[]{:S(2)}, u32[]{:S(2)}) collective-permute-start(bf16[2,256,128]{2,1,0:T(8,128)(2,1)} %collective-permute-done.2), channel_id=1, source_target_pairs={{0,4},{4,8},{8,12},{12,16},{16,20},{20,24},{24,28},{28,32},{32,36}... | collective-permute-start | bytes 393224 | tf_op jit(solution)/shard_map/ppermute | solution.py:18
  48.3 1.1 mul.394
  49.7 0.9 constant_dynamic-update-slice_fusion.4
  50.6 0.9 constant_dynamic-update-slice_fusion.3
  51.5 0.9 constant_dynamic-update-slice_fusion.2
  52.5 0.9 constant_dynamic-update-slice_fusion.1
  53.6 1.3 reshape.600
  54.9 1.2 reshape.602
  56.1 57.9 %while.15 = (s32[]{:T(128)}, f32[4,512,128]{2,1,0:T(8,128)}, f32[4,1280,128]{2,1,0:T(8,128)}, f32[4,1280,128]{2,1,0:T(8,128)}, bf16[4,512,128]{2,1,0:T(8,128)(2,...) while((s32[]{:T(128)}, f32[4,512,128]{2,1,0:T(8,128)}, ...), condition=%wide.region_10.11_spmd.clone, body=%wide.region_6.10_spmd.clone.sunk | while | flops 1015675904 | bytes 32867196 | solution.py:115
  56.9 1.7 fusion.108
  59.1 1.6 fusion.109
  60.8 2.0 fusion.110
  62.8 1.8 fusion.111
  64.7 1.4 fusion.113
  66.0 2.3 fusion.114
  68.3 2.2 fusion.112
  71.4 1.7 fusion.108
  73.6 1.6 fusion.109
  75.3 2.0 fusion.110
  77.3 1.8 fusion.111
  79.1 1.4 fusion.113
  80.5 2.3 fusion.114
  82.8 2.2 fusion.112
  85.8 1.7 fusion.108
  88.1 1.6 fusion.109
  89.8 2.0 fusion.110
  91.8 1.8 fusion.111
  93.6 1.4 fusion.113
  95.0 2.3 fusion.114
  97.3 2.2 fusion.112
  100.3 1.7 fusion.108
  102.6 1.6 fusion.109
  104.3 2.0 fusion.110
  106.2 1.8 fusion.111
  108.1 1.4 fusion.113
  109.5 2.3 fusion.114
  111.8 2.2 fusion.112
  114.0 2.0 reduce_sum.120
  115.9 2.0 reduce_sum.121
  118.0 1.3 collective-permute-start.4
  119.3 0.8 copy.20
  120.8 5.3 %collective-permute-done.4 = bf16[2,256,128]{2,1,0:T(8,128)(2,1)S(1)} collective-permute-done((bf16[2,256,128]{2,1,0:T(8,128)(2,1)S(1)}, bf16[2,256,128]{2,1,0:T(8,128)(2,1)S(1)}, u32[]{:S(2)}, u32[]{:S(2)}) %collective-permute-start.4) | collective-permute-done | bytes 131104 | tf_op jit(solution)/shard_map/ppermute | solution.py:18
  126.1 1.5 collective-permute-start.5
  127.6 0.9 multiply_reduce_fusion.1
  128.5 6.6 %collective-permute-done.5 = bf16[2,256,128]{2,1,0:T(8,128)(2,1)S(1)} collective-permute-done((bf16[2,256,128]{2,1,0:T(8,128)(2,1)S(1)}, bf16[2,256,128]{2,1,0:T(8,128)(2,1)S(1)}, u32[]{:S(2)}, u32[]{:S(2)}) %collective-permute-start.5) | collective-permute-done | bytes 131104 | tf_op jit(solution)/shard_map/ppermute | solution.py:18
  135.1 1.3 collective-permute-start.6
  136.8 1.2 mul.399
  138.0 1.1 concatenate.76
  139.1 6.0 %collective-permute-done.6 = bf16[2,256,128]{2,1,0:T(8,128)(2,1)} collective-permute-done((bf16[2,256,128]{2,1,0:T(8,128)(2,1)S(1)}, bf16[2,256,128]{2,1,0:T(8,128)(2,1)}, u32[]{:S(2)}, u32[]{:S(2)}) %collective-permute-start.6) | collective-permute-done | bytes 131104 | tf_op jit(solution)/shard_map/ppermute | solution.py:18
  145.1 0.9 fusion.28
  146.1 1.4 collective-permute-start.7
  147.6 2.9 %multiply_reduce_fusion = (f32[1024]{0:T(1024)S(1)}, bf16[1,256,1024]{2,1,0:T(8,128)(2,1)}) fusion(f32[1,256,1024]{2,1,0:T(8,128)} %concatenate.76, f32[1,256,1024]{2,1,0:T(8,128)S(1)} %copy-done.5, bf16[1,256,1024]{2,1,0:T(8,128)(2,1)} %param.9, f32[1,256,1024]{2,1,0:T(8,128)} %mul.399, f32[1024]{0:T(1024)S(1)} %copy-done.30), kind=kLoop, calls=%fused_computation.47 | loop fusion | flops 2358272 | bytes 4202496 | tf_op jit(solution)/shard_map/reduce_sum | solution.py:62
  150.5 6.5 %collective-permute-done.7 = bf16[2,256,128]{2,1,0:T(8,128)(2,1)S(1)} collective-permute-done((bf16[2,256,128]{2,1,0:T(8,128)(2,1)S(1)}, bf16[2,256,128]{2,1,0:T(8,128)(2,1)S(1)}, u32[]{:S(2)}, u32[]{:S(2)}) %collective-permute-start.7) | collective-permute-done | bytes 131104 | tf_op jit(solution)/shard_map/ppermute | solution.py:18
  158.5 113.9 %psum.7 = f32[2,128]{1,0:T(2,128)S(1)} all-reduce(f32[2,128]{1,0:T(2,128)S(1)} %pad_maximum_fusion.5), channel_id=1, replica_groups=mesh['dp'=4,'ctx'=32,'tp'=4] {'dp','ctx','tp'}, use_global_device_ids=true, to_apply=%region_18.19 | all-reduce | flops 256 | bytes 2048 | tf_op jit(solution)/shard_map/psum | solution.py:192
  (196 shorter events, 15.7 us)
Async XLA Ops:
  0.6 13.9 %copy-start.32 = (f32[64]{0:T(128)}, f32[64]{0:T(128)S(1)}, u32[]{:S(2)}) copy-start(f32[64]{0:T(128)S(1)} %multiply_exponential_fusion) | copy-start | bytes 772
  3.2 11.7 %copy-start.26 = (f32[256]{0:T(256)}, f32[256]{0:T(256)S(1)}, u32[]{:S(2)}) copy-start(f32[256]{0:T(256)S(1)} %add_rsqrt_fusion.1) | copy-start | bytes 3076
  3.3 11.6 %copy-start.28 = (f32[256]{0:T(256)}, f32[256]{0:T(256)S(1)}, u32[]{:S(2)}) copy-start(f32[256]{0:T(256)S(1)} %get-tuple-element.134) | copy-start | bytes 3076
  4.9 7.7 %copy-start.12 = (bf16[1,256,64]{2,1,0:T(8,128)(2,1)}, bf16[1,256,64]{2,1,0:T(8,128)(2,1)S(1)}, u32[]{:S(2)}) copy-start(bf16[1,256,64]{2,1,0:T(8,128)(2,1)S(1)} %get-tuple-element.130) | copy-start | bytes 98308
  4.9 7.7 %copy-start.14 = (bf16[1,256,64]{2,1,0:T(8,128)(2,1)}, bf16[1,256,64]{2,1,0:T(8,128)(2,1)S(1)}, u32[]{:S(2)}) copy-start(bf16[1,256,64]{2,1,0:T(8,128)(2,1)S(1)} %get-tuple-element.131) | copy-start | bytes 98308
  5.9 10.5 %collective-permute-start = (bf16[2,256,128]{2,1,0:T(8,128)(2,1)S(1)}, bf16[2,256,128]{2,1,0:T(8,128)(2,1)S(1)}, u32[]{:S(2)}, u32[]{:S(2)}) collective-permute-start(bf16[2,256,128]{2,1,0:T(8,128)(2,1)S(1)} %pad_maximum_fusion.3), channel_id=1, source_target_pairs={{0,4},{4,8},{8,12},{12,16},{16,20},{20,24},{24,28},{28,32},{32,36}... | collective-permute-start | bytes 393224 | tf_op jit(solution)/shard_map/ppermute | solution.py:18
  13.1 2.8 %copy-start.6 = (f32[256,64]{1,0:T(8,128)}, f32[256,64]{1,0:T(8,128)S(1)}, u32[]{:S(2)}) copy-start(f32[256,64]{1,0:T(8,128)S(1)} %get-tuple-element.132) | copy-start | bytes 196612
  13.1 2.8 %copy-start.8 = (f32[256,64]{1,0:T(8,128)}, f32[256,64]{1,0:T(8,128)S(1)}, u32[]{:S(2)}) copy-start(f32[256,64]{1,0:T(8,128)S(1)} %get-tuple-element.133) | copy-start | bytes 196612
  13.1 2.4 copy-start.34
  14.6 1.0 copy-start.1
  15.9 31.6 %copy-start.16 = (bf16[1,256,1024]{2,1,0:T(8,128)(2,1)S(1)}, bf16[1,256,1024]{2,1,0:T(8,128)(2,1)}, u32[]{:S(2)}) copy-start(bf16[1,256,1024]{2,1,0:T(8,128)(2,1)} %param.12) | copy-start | bytes 1572868
  16.4 31.4 %copy-start.20 = (bf16[2,256,128]{2,1,0:T(8,128)(2,1)}, bf16[2,256,128]{2,1,0:T(8,128)(2,1)S(1)}, u32[]{:S(2)}) copy-start(bf16[2,256,128]{2,1,0:T(8,128)(2,1)S(1)} %collective-permute-done) | copy-start | bytes 393220
  16.4 11.0 %collective-permute-start.1 = (bf16[2,256,128]{2,1,0:T(8,128)(2,1)S(1)}, bf16[2,256,128]{2,1,0:T(8,128)(2,1)S(1)}, u32[]{:S(2)}, u32[]{:S(2)}) collective-permute-start(bf16[2,256,128]{2,1,0:T(8,128)(2,1)S(1)} %collective-permute-done), channel_id=1, source_target_pairs={{0,4},{4,8},{8,12},{12,16},{16,20},{20,24},{24,28},{28,32},{32,36}... | collective-permute-start | bytes 393224 | tf_op jit(solution)/shard_map/ppermute | solution.py:18
  27.4 20.5 %copy-start.21 = (bf16[2,256,128]{2,1,0:T(8,128)(2,1)}, bf16[2,256,128]{2,1,0:T(8,128)(2,1)S(1)}, u32[]{:S(2)}) copy-start(bf16[2,256,128]{2,1,0:T(8,128)(2,1)S(1)} %collective-permute-done.1) | copy-start | bytes 393220
  27.4 11.0 %collective-permute-start.2 = (bf16[2,256,128]{2,1,0:T(8,128)(2,1)S(1)}, bf16[2,256,128]{2,1,0:T(8,128)(2,1)}, u32[]{:S(2)}, u32[]{:S(2)}) collective-permute-start(bf16[2,256,128]{2,1,0:T(8,128)(2,1)S(1)} %collective-permute-done.1), channel_id=1, source_target_pairs={{0,4},{4,8},{8,12},{12,16},{16,20},{20,24},{24,28},{28,32},{32,36}... | collective-permute-start | bytes 393224 | tf_op jit(solution)/shard_map/ppermute | solution.py:18
  38.4 11.3 %collective-permute-start.3 = (bf16[2,256,128]{2,1,0:T(8,128)(2,1)}, bf16[2,256,128]{2,1,0:T(8,128)(2,1)}, u32[]{:S(2)}, u32[]{:S(2)}) collective-permute-start(bf16[2,256,128]{2,1,0:T(8,128)(2,1)} %collective-permute-done.2), channel_id=1, source_target_pairs={{0,4},{4,8},{8,12},{12,16},{16,20},{20,24},{24,28},{28,32},{32,36}... | collective-permute-start | bytes 393224 | tf_op jit(solution)/shard_map/ppermute | solution.py:18
  48.2 5.2 %copy-start.13 = (bf16[1,256,64]{2,1,0:T(8,128)(2,1)S(1)}, bf16[1,256,64]{2,1,0:T(8,128)(2,1)}, u32[]{:S(2)}) copy-start(bf16[1,256,64]{2,1,0:T(8,128)(2,1)} %copy-done.12) | copy-start | bytes 98308
  48.3 5.2 %copy-start.15 = (bf16[1,256,64]{2,1,0:T(8,128)(2,1)S(1)}, bf16[1,256,64]{2,1,0:T(8,128)(2,1)}, u32[]{:S(2)}) copy-start(bf16[1,256,64]{2,1,0:T(8,128)(2,1)} %copy-done.14) | copy-start | bytes 98308
  48.3 5.2 %copy-start.19 = (bf16[1,256,128]{2,1,0:T(8,128)(2,1)S(1)}, bf16[1,256,128]{2,1,0:T(8,128)(2,1)}, u32[]{:S(2)}) copy-start(bf16[1,256,128]{2,1,0:T(8,128)(2,1)} %param.11) | copy-start | bytes 196612
  56.1 2.5 copy-start.22
  56.1 3.0 %copy-start.24 = (s32[256]{0:T(256)}, s32[256]{0:T(256)S(1)}, u32[]{:S(2)}) copy-start(s32[256]{0:T(256)S(1)} %get-tuple-element.251) | copy-start | bytes 3076 | tf_op jit(solution)/shard_map/while
  62.8 3.3 %copy-start = (bf16[2,256,1280]{2,1,0:T(8,128)(2,1)S(1)}, bf16[2,256,1280]{2,1,0:T(8,128)(2,1)}, u32[]{:S(2)}) copy-start(bf16[2,256,1280]{2,1,0:T(8,128)(2,1)} %fusion.109) | copy-start | bytes 3932164 | tf_op jit(solution)/shard_map/while
  64.6 5.9 %copy-start.4 = (bf16[4,512,128]{2,1,0:T(8,128)(2,1)S(1)}, bf16[4,512,128]{2,1,0:T(8,128)(2,1)}, u32[]{:S(2)}) copy-start(bf16[4,512,128]{2,1,0:T(8,128)(2,1)} %copy-done.3) | copy-start | bytes 1572868 | tf_op jit(solution)/shard_map/while
  64.6 5.9 %copy-start.18 = (s32[1280]{0:T(1024)S(1)}, s32[1280]{0:T(1024)}, u32[]{:S(2)}) copy-start(s32[1280]{0:T(1024)} %copy-done.17) | copy-start | bytes 15364 | tf_op jit(solution)/shard_map/while
  64.6 5.9 %copy-start.23 = (s32[256]{0:T(256)S(1)}, s32[256]{0:T(256)}, u32[]{:S(2)}) copy-start(s32[256]{0:T(256)} %copy-done.22) | copy-start | bytes 3076 | tf_op jit(solution)/shard_map/while
  64.6 5.9 %copy-start.25 = (s32[256]{0:T(256)S(1)}, s32[256]{0:T(256)}, u32[]{:S(2)}) copy-start(s32[256]{0:T(256)} %copy-done.24) | copy-start | bytes 3076 | tf_op jit(solution)/shard_map/while
  70.6 0.8 copy-start.3
  70.6 2.5 copy-start.22
  70.6 3.0 %copy-start.24 = (s32[256]{0:T(256)}, s32[256]{0:T(256)S(1)}, u32[]{:S(2)}) copy-start(s32[256]{0:T(256)S(1)} %get-tuple-element.251) | copy-start | bytes 3076 | tf_op jit(solution)/shard_map/while
  77.3 3.3 %copy-start = (bf16[2,256,1280]{2,1,0:T(8,128)(2,1)S(1)}, bf16[2,256,1280]{2,1,0:T(8,128)(2,1)}, u32[]{:S(2)}) copy-start(bf16[2,256,1280]{2,1,0:T(8,128)(2,1)} %fusion.109) | copy-start | bytes 3932164 | tf_op jit(solution)/shard_map/while
  79.1 5.9 %copy-start.4 = (bf16[4,512,128]{2,1,0:T(8,128)(2,1)S(1)}, bf16[4,512,128]{2,1,0:T(8,128)(2,1)}, u32[]{:S(2)}) copy-start(bf16[4,512,128]{2,1,0:T(8,128)(2,1)} %copy-done.3) | copy-start | bytes 1572868 | tf_op jit(solution)/shard_map/while
  79.1 5.9 %copy-start.18 = (s32[1280]{0:T(1024)S(1)}, s32[1280]{0:T(1024)}, u32[]{:S(2)}) copy-start(s32[1280]{0:T(1024)} %copy-done.17) | copy-start | bytes 15364 | tf_op jit(solution)/shard_map/while
  79.1 5.9 %copy-start.23 = (s32[256]{0:T(256)S(1)}, s32[256]{0:T(256)}, u32[]{:S(2)}) copy-start(s32[256]{0:T(256)} %copy-done.22) | copy-start | bytes 3076 | tf_op jit(solution)/shard_map/while
  79.1 5.9 %copy-start.25 = (s32[256]{0:T(256)S(1)}, s32[256]{0:T(256)}, u32[]{:S(2)}) copy-start(s32[256]{0:T(256)} %copy-done.24) | copy-start | bytes 3076 | tf_op jit(solution)/shard_map/while
  85.1 2.5 copy-start.22
  85.1 3.0 %copy-start.24 = (s32[256]{0:T(256)}, s32[256]{0:T(256)S(1)}, u32[]{:S(2)}) copy-start(s32[256]{0:T(256)S(1)} %get-tuple-element.251) | copy-start | bytes 3076 | tf_op jit(solution)/shard_map/while
  91.8 3.3 %copy-start = (bf16[2,256,1280]{2,1,0:T(8,128)(2,1)S(1)}, bf16[2,256,1280]{2,1,0:T(8,128)(2,1)}, u32[]{:S(2)}) copy-start(bf16[2,256,1280]{2,1,0:T(8,128)(2,1)} %fusion.109) | copy-start | bytes 3932164 | tf_op jit(solution)/shard_map/while
  93.6 5.9 %copy-start.4 = (bf16[4,512,128]{2,1,0:T(8,128)(2,1)S(1)}, bf16[4,512,128]{2,1,0:T(8,128)(2,1)}, u32[]{:S(2)}) copy-start(bf16[4,512,128]{2,1,0:T(8,128)(2,1)} %copy-done.3) | copy-start | bytes 1572868 | tf_op jit(solution)/shard_map/while
  93.6 5.9 %copy-start.18 = (s32[1280]{0:T(1024)S(1)}, s32[1280]{0:T(1024)}, u32[]{:S(2)}) copy-start(s32[1280]{0:T(1024)} %copy-done.17) | copy-start | bytes 15364 | tf_op jit(solution)/shard_map/while
  93.6 5.9 %copy-start.23 = (s32[256]{0:T(256)S(1)}, s32[256]{0:T(256)}, u32[]{:S(2)}) copy-start(s32[256]{0:T(256)} %copy-done.22) | copy-start | bytes 3076 | tf_op jit(solution)/shard_map/while
  93.6 5.9 %copy-start.25 = (s32[256]{0:T(256)S(1)}, s32[256]{0:T(256)}, u32[]{:S(2)}) copy-start(s32[256]{0:T(256)} %copy-done.24) | copy-start | bytes 3076 | tf_op jit(solution)/shard_map/while
  99.5 2.5 copy-start.22
  99.6 3.0 %copy-start.24 = (s32[256]{0:T(256)}, s32[256]{0:T(256)S(1)}, u32[]{:S(2)}) copy-start(s32[256]{0:T(256)S(1)} %get-tuple-element.251) | copy-start | bytes 3076 | tf_op jit(solution)/shard_map/while
  106.2 3.3 %copy-start = (bf16[2,256,1280]{2,1,0:T(8,128)(2,1)S(1)}, bf16[2,256,1280]{2,1,0:T(8,128)(2,1)}, u32[]{:S(2)}) copy-start(bf16[2,256,1280]{2,1,0:T(8,128)(2,1)} %fusion.109) | copy-start | bytes 3932164 | tf_op jit(solution)/shard_map/while
  108.1 5.9 %copy-start.4 = (bf16[4,512,128]{2,1,0:T(8,128)(2,1)S(1)}, bf16[4,512,128]{2,1,0:T(8,128)(2,1)}, u32[]{:S(2)}) copy-start(bf16[4,512,128]{2,1,0:T(8,128)(2,1)} %copy-done.3) | copy-start | bytes 1572868 | tf_op jit(solution)/shard_map/while
  108.1 5.9 %copy-start.18 = (s32[1280]{0:T(1024)S(1)}, s32[1280]{0:T(1024)}, u32[]{:S(2)}) copy-start(s32[1280]{0:T(1024)} %copy-done.17) | copy-start | bytes 15364 | tf_op jit(solution)/shard_map/while
  108.1 5.9 %copy-start.23 = (s32[256]{0:T(256)S(1)}, s32[256]{0:T(256)}, u32[]{:S(2)}) copy-start(s32[256]{0:T(256)} %copy-done.22) | copy-start | bytes 3076 | tf_op jit(solution)/shard_map/while
  108.1 5.9 %copy-start.25 = (s32[256]{0:T(256)S(1)}, s32[256]{0:T(256)}, u32[]{:S(2)}) copy-start(s32[256]{0:T(256)} %copy-done.24) | copy-start | bytes 3076 | tf_op jit(solution)/shard_map/while
  115.9 3.4 %copy-start.11 = (f32[4,512,128]{2,1,0:T(8,128)S(1)}, f32[4,512,128]{2,1,0:T(8,128)}, u32[]{:S(2)}) copy-start(f32[4,512,128]{2,1,0:T(8,128)} %get-tuple-element.53) | copy-start | bytes 3145732
  115.9 4.2 %copy-start.7 = (f32[256,64]{1,0:T(8,128)S(1)}, f32[256,64]{1,0:T(8,128)}, u32[]{:S(2)}) copy-start(f32[256,64]{1,0:T(8,128)} %copy-done.6) | copy-start | bytes 196612
  115.9 4.2 %copy-start.9 = (f32[256,64]{1,0:T(8,128)S(1)}, f32[256,64]{1,0:T(8,128)}, u32[]{:S(2)}) copy-start(f32[256,64]{1,0:T(8,128)} %copy-done.8) | copy-start | bytes 196612
  118.0 8.0 %collective-permute-start.4 = (bf16[2,256,128]{2,1,0:T(8,128)(2,1)S(1)}, bf16[2,256,128]{2,1,0:T(8,128)(2,1)S(1)}, u32[]{:S(2)}, u32[]{:S(2)}) collective-permute-start(bf16[2,256,128]{2,1,0:T(8,128)(2,1)S(1)} %fusion.67), channel_id=1, source_target_pairs={{4,0},{8,4},{12,8},{16,12},{20,16},{24,20},{28,24},{32,28},{36,32}... | collective-permute-start | bytes 393224 | tf_op jit(solution)/shard_map/ppermute | solution.py:18
  120.2 7.4 %copy-start.2 = (f32[32,8,8,128]{3,2,1,0:T(8,128)S(1)}, f32[32,8,8,128]{3,2,1,0:T(8,128)}, u32[]{:S(2)}) copy-start(f32[32,8,8,128]{3,2,1,0:T(8,128)} %copy-done.1) | copy-start | bytes 3145732
  120.2 7.4 %copy-start.35 = (f32[128]{0:T(128)S(1)}, f32[128]{0:T(128)}, u32[]{:S(2)}) copy-start(f32[128]{0:T(128)} %param.13) | copy-start | bytes 1540
  126.1 9.0 %collective-permute-start.5 = (bf16[2,256,128]{2,1,0:T(8,128)(2,1)S(1)}, bf16[2,256,128]{2,1,0:T(8,128)(2,1)S(1)}, u32[]{:S(2)}, u32[]{:S(2)}) collective-permute-start(bf16[2,256,128]{2,1,0:T(8,128)(2,1)S(1)} %fusion.34), channel_id=1, source_target_pairs={{4,0},{8,4},{12,8},{16,12},{20,16},{24,20},{28,24},{32,28},{36,32}... | collective-permute-start | bytes 393224 | tf_op jit(solution)/shard_map/ppermute | solution.py:18
  135.1 10.0 %collective-permute-start.6 = (bf16[2,256,128]{2,1,0:T(8,128)(2,1)S(1)}, bf16[2,256,128]{2,1,0:T(8,128)(2,1)}, u32[]{:S(2)}, u32[]{:S(2)}) collective-permute-start(bf16[2,256,128]{2,1,0:T(8,128)(2,1)S(1)} %fusion.38), channel_id=1, source_target_pairs={{4,0},{8,4},{12,8},{16,12},{20,16},{24,20},{28,24},{32,28},{36,32}... | collective-permute-start | bytes 393224 | tf_op jit(solution)/shard_map/ppermute | solution.py:18
  136.8 10.8 %copy-start.30 = (f32[1024]{0:T(1024)S(1)}, f32[1024]{0:T(1024)}, u32[]{:S(2)}) copy-start(f32[1024]{0:T(1024)} %broadcast_bitcast_fusion) | copy-start | bytes 12292
  138.0 9.6 %copy-start.5 = (f32[1,256,1024]{2,1,0:T(8,128)S(1)}, f32[1,256,1024]{2,1,0:T(8,128)}, u32[]{:S(2)}) copy-start(f32[1,256,1024]{2,1,0:T(8,128)} %mul.394) | copy-start | bytes 3145732
  146.0 11.7 %copy-start.29 = (f32[256]{0:T(256)S(1)}, f32[256]{0:T(256)}, u32[]{:S(2)}) copy-start(f32[256]{0:T(256)} %copy-done.28) | copy-start | bytes 3076
  146.1 11.6 %copy-start.33 = (f32[64]{0:T(128)S(1)}, f32[64]{0:T(128)}, u32[]{:S(2)}) copy-start(f32[64]{0:T(128)} %copy-done.32) | copy-start | bytes 772
  146.1 12.2 %copy-start.10 = (bf16[1,256,128]{2,1,0:T(8,128)(2,1)S(1)}, bf16[1,256,128]{2,1,0:T(8,128)(2,1)}, u32[]{:S(2)}) copy-start(bf16[1,256,128]{2,1,0:T(8,128)(2,1)} %param.10) | copy-start | bytes 196612
  146.1 12.2 %copy-start.27 = (f32[256]{0:T(256)S(1)}, f32[256]{0:T(256)}, u32[]{:S(2)}) copy-start(f32[256]{0:T(256)} %copy-done.26) | copy-start | bytes 3076
  146.1 12.2 %copy-start.31 = (f32[128]{0:T(128)S(1)}, f32[128]{0:T(128)}, u32[]{:S(2)}) copy-start(f32[128]{0:T(128)} %param.14) | copy-start | bytes 1540
  146.1 10.9 %collective-permute-start.7 = (bf16[2,256,128]{2,1,0:T(8,128)(2,1)S(1)}, bf16[2,256,128]{2,1,0:T(8,128)(2,1)S(1)}, u32[]{:S(2)}, u32[]{:S(2)}) collective-permute-start(bf16[2,256,128]{2,1,0:T(8,128)(2,1)S(1)} %fusion.28), channel_id=1, source_target_pairs={{4,0},{8,4},{12,8},{16,12},{20,16},{24,20},{28,24},{32,28},{36,32}... | collective-permute-start | bytes 393224 | tf_op jit(solution)/shard_map/ppermute | solution.py:18
  (7 other events, 5.5 us)
where the time goes:
time: 275 us; the launch traced here: 274 us
  blocking collectives  114 us (41%)
  matrix products  45.3 us (16%)
  starting transfers between devices  38.9 us (14%)
  other arithmetic  29.9 us (11%)
  waiting for transfers between devices  27.8 us (10%)
  local copies, waits for them, and re-layouts  16.1 us (6%)
    psum x1, blocking collectives, on_device(): lax.psum(jnp.stack([q_term, k_term]), ('dp', 'ctx', 'tp')) * loss_scale  114 us
    ppermute x8, starting transfers between devices, shifted(): return lax.ppermute(block, axis, route)  38.9 us
    ppermute x8, waiting for transfers between devices, shifted(): return lax.ppermute(block, axis, route)  27.8 us
    dot_general x4, matrix products, one_unit(): v_grad = jnp.dot(weights_b.T, gradient, preferred_element_type=jnp.float32)  9.16 us
    dot_general x4, matrix products, one_unit(): q_grad = jnp.dot(score_grad, keyset, preferred_element_type=jnp.float32)  8.69 us
    dot_general x4, matrix products, one_unit(): attn_out = jnp.dot(weights_b, valueset, preferred_element_type=jnp.float32)  7.81 us
    dot_general x4, matrix products, one_unit(): jnp.dot(gradient, valueset.T, preferred_element_type=jnp.float32)  7.21 us
    dot_general x4, matrix products, one_unit(): jnp.dot(queries, keyset.T, preferred_element_type=jnp.float32)  6.86 us
  transfers between devices with their start and end apart: 8, of which 6 were waited for; matrix products, arithmetic and copies ran while one was open for 5% of the time, Pallas kernels for 0%

commit v1 on v0

v1 whole, which is shorter than its diff:
```python
import functools
import math

import jax
import jax.numpy as jnp
import numpy as np
from jax import lax
from jax.experimental import pallas as pl
from jax.experimental.pallas import tpu as pltpu
from jax.sharding import Mesh
from jax.sharding import PartitionSpec as P

REACH = 4
EPSILON = 1e-06
ROPE_BASE = 1000000.0
HD = 128
HALF = HD // 2
BLOCKS = REACH + 1
HEADS_PER_STEP = 2
MASKED = -1e30
LOG2E = 1.4426950408889634


def rope_tables(rows):
    freq = ROPE_BASE ** (-2.0 * np.arange(HALF, dtype=np.float64) / HD)
    offsets = np.concatenate([np.arange(rows) - rows * d for d in range(1, REACH + 1)])
    angles = offsets[:, None].astype(np.float64) * np.concatenate([freq, freq])[None, :]
    return np.cos(angles).astype(np.float32), np.sin(angles).astype(np.float32)


def half_sign():
    lane = lax.broadcasted_iota(jnp.int32, (1, HD), 1)
    return jnp.where(lane < HALF, -1.0, 1.0).astype(jnp.float32)


def prep_kernel(rows, docs, lens_ref, first_ref, freq_ref, tabc_ref, tabs_ref, cos_ref, sin_ref, low_ref, scal_ref):
    first = first_ref[0]
    tok_col = lax.broadcasted_iota(jnp.int32, (rows, HD), 0)
    tok_row = lax.broadcasted_iota(jnp.int32, (8, rows), 1)

    def one_doc(d, carry):
        start, reaching, col, row = carry
        rel = start - first
        reaching = jnp.where(rel <= 0, rel, reaching)
        col = jnp.where(tok_col >= rel, rel, col)
        row = jnp.where(tok_row >= rel, rel, row)
        return start + lens_ref[0, d], reaching, col, row

    zero = jnp.int32(0)
    _, reaching, col, row = lax.fori_loop(
        0, docs, one_doc, (zero, zero, jnp.zeros((rows, HD), jnp.int32), jnp.zeros((8, rows), jnp.int32))
    )
    before = -reaching
    scal_ref[0] = before
    scal_ref[1] = 1 + (before + rows - 1) // rows
    low_ref[...] = row
    sign = half_sign()
    freq = freq_ref[...]
    angles = (tok_col - col).astype(jnp.float32) * freq
    cos_ref[0:rows, :] = jnp.cos(angles)
    sin_ref[0:rows, :] = jnp.sin(angles) * sign
    shift = before.astype(jnp.float32) * freq
    shift_c, shift_s = jnp.cos(shift), jnp.sin(shift)
    tab_c, tab_s = tabc_ref[...], tabs_ref[...]
    cos_ref[rows:, :] = shift_c * tab_c - shift_s * tab_s
    sin_ref[rows:, :] = (shift_s * tab_c + shift_c * tab_s) * sign


def normed_of(source):
    values32 = source.astype(jnp.float32)
    inv = lax.rsqrt(jnp.mean(values32 * values32, axis=-1, keepdims=True) + EPSILON)
    return values32 * inv, inv


def rope(scaled, cos, sin):
    return scaled * cos + pltpu.roll(scaled, HALF, 1) * sin


def unrope(grad, cos, sin):
    return grad * cos - pltpu.roll(grad, HALF, 1) * sin


def fold(terms):
    return jnp.sum(terms.reshape(terms.shape[0] // 8, 8, HD), axis=0)


def main_kernel(
    rows, fan,
    scal_ref, low_ref, cos_ref, sin_ref, qgain_ref, kgain_ref, w0, w1, w2, w3, w4, q_ref, g_ref,
    dq_ref, own_ref, o1, o2, o3, o4, gains_ref,
    krot, vwin, knorm, bias, dk, dv, qterm,
):
    step = pl.program_id(0)
    count = scal_ref[1]
    window = (w0, w1, w2, w3, w4)
    heads = q_ref.shape[1] // HD
    scale = HD ** (-0.5)

    @pl.when(step == 0)
    def _():
        qterm[...] = jnp.zeros_like(qterm)
        for d in range(BLOCKS):
            at = slice(d * rows, (d + 1) * rows)

            @pl.when(d < count)
            def _():
                normed, _ = normed_of(window[d][:, :HD])
                knorm[at, :] = normed
                krot[at, :] = rope(normed * kgain_ref[...], cos_ref[at, :], sin_ref[at, :]).astype(jnp.bfloat16)
                vwin[at, :] = window[d][:, HD:]
                dk[at, :] = jnp.zeros((rows, HD), jnp.float32)
                dv[at, :] = jnp.zeros((rows, HD), jnp.float32)
                key = lax.broadcasted_iota(jnp.int32, (rows, rows), 0) - d * rows
                tok = lax.broadcasted_iota(jnp.int32, (rows, rows), 1)
                kept = key >= low_ref[0:1, :]
                if d == 0:
                    kept = kept & (key <= tok)
                bias[at, :] = jnp.where(kept, 0.0, MASKED)

    def attend(blocks):
        size = blocks * rows
        for h in range(heads):
            lanes = slice(h * HD, (h + 1) * HD)
            cos, sin = cos_ref[0:rows, :], sin_ref[0:rows, :]
            q_normed, q_inv = normed_of(q_ref[:, lanes])
            q_rot = rope(q_normed * qgain_ref[...], cos, sin).astype(jnp.bfloat16)
            grad = g_ref[:, lanes]
            keys, vals = krot[0:size, :], vwin[0:size, :]
            across = (((1,), (1,)), ((), ()))
            scores = lax.dot_general(keys, q_rot, across, preferred_element_type=jnp.float32) + bias[0:size, :]
            top = jnp.max(scores, axis=0, keepdims=True)
            power = jnp.exp2((scores - top) * (scale * LOG2E))
            inv_sum = 1.0 / jnp.sum(power, axis=0, keepdims=True)
            wgrad = lax.dot_general(vals, grad, across, preferred_element_type=jnp.float32)
            delta = jnp.sum(power * wgrad, axis=0, keepdims=True) * inv_sum
            weights = power * inv_sum
            sgrad = (weights * (wgrad - delta)).astype(jnp.bfloat16)
            dv[0:size, :] += jnp.dot(weights.astype(jnp.bfloat16), grad, preferred_element_type=jnp.float32)
            dk[0:size, :] += jnp.dot(sgrad, q_rot, preferred_element_type=jnp.float32)
            q_grad = lax.dot_general(sgrad, keys, (((0,), (0,)), ((), ())), preferred_element_type=jnp.float32)
            norm_grad = unrope(q_grad * scale, cos, sin)
            qterm[...] += fold(norm_grad * q_normed)
            gained = norm_grad * qgain_ref[...]
            mean = jnp.mean(gained * q_normed, axis=-1, keepdims=True)
            dq_ref[:, lanes] = ((gained - q_normed * mean) * q_inv).astype(jnp.bfloat16)

    for blocks in range(1, BLOCKS + 1):
        pl.when(count == blocks)(functools.partial(attend, blocks))

    @pl.when(step == pl.num_programs(0) - 1)
    def _():
        kterm = jnp.zeros((8, HD), jnp.float32)
        outs = (own_ref, o1, o2, o3, o4)
        for d in range(BLOCKS):
            at = slice(d * rows, (d + 1) * rows)

            def block_term():
                key_grad = dk[at, :] * scale
                outs[d][:, :HD] = key_grad.astype(outs[d].dtype)
                outs[d][:, HD:] = dv[at, :].astype(outs[d].dtype)
                norm_grad = unrope(key_grad, cos_ref[at, :], sin_ref[at, :])
                return fold(norm_grad * knorm[at, :])

            def no_term():
                outs[d][...] = jnp.zeros_like(outs[d])
                return jnp.zeros((8, HD), jnp.float32)

            kterm = kterm + (block_term() if d == 0 else lax.cond(d < count, block_term, no_term))
        both = jnp.concatenate(
            [jnp.sum(qterm[...], axis=0, keepdims=True), jnp.sum(kterm, axis=0, keepdims=True)], axis=0
        )
        gains_ref[...] = jnp.broadcast_to(both[None], (fan, 2, HD))


def final_kernel(rows, own_ref, r1, r2, r3, r4, kv_ref, kgain_ref, cos_ref, sin_ref, dk_ref, dv_ref):
    total = own_ref[...]
    for part in (r1, r2, r3, r4):
        total = total + part[...].astype(jnp.float32)
    dv_ref[...] = total[:, HD:].astype(jnp.bfloat16)
    normed, inv = normed_of(kv_ref[:, :HD])
    gained = unrope(total[:, :HD], cos_ref[0:rows, :], sin_ref[0:rows, :]) * kgain_ref[...]
    mean = jnp.mean(gained * normed, axis=-1, keepdims=True)
    dk_ref[...] = ((gained - normed * mean) * inv).astype(jnp.bfloat16)


VMEM = pl.BlockSpec(memory_space=pltpu.VMEM)
SMEM = pl.BlockSpec(memory_space=pltpu.SMEM)
LIMIT = pltpu.CompilerParams(vmem_limit_bytes=40 * 1024 * 1024)


def prepare(doc_lengths, first, rows):
    docs = doc_lengths.shape[1]
    half = jnp.exp(jnp.arange(HALF, dtype=jnp.float32) * (-2.0 * math.log(ROPE_BASE) / HD))
    freq = jnp.concatenate([half, half])[None]
    tab_c, tab_s = rope_tables(rows)
    table = jax.ShapeDtypeStruct((BLOCKS * rows, HD), jnp.float32)
    return pl.pallas_call(
        functools.partial(prep_kernel, rows, docs),
        in_specs=[SMEM, SMEM, VMEM, VMEM, VMEM],
        out_specs=[VMEM, VMEM, VMEM, SMEM],
        out_shape=[
            table,
            table,
            jax.ShapeDtypeStruct((8, rows), jnp.int32),
            jax.ShapeDtypeStruct((2,), jnp.int32),
        ],
        compiler_params=LIMIT,
        name="prep",
    )(doc_lengths, first, freq, tab_c, tab_s)


def attention(scal, low, cos, sin, q_gain, k_gain, window, queries, grads, fan):
    rows, width = queries.shape
    step_width = HEADS_PER_STEP * HD
    by_head = pl.BlockSpec((rows, step_width), lambda i: (0, i))
    size = BLOCKS * rows
    part = jax.ShapeDtypeStruct((rows, 2 * HD), jnp.bfloat16)
    return pl.pallas_call(
        functools.partial(main_kernel, rows, fan),
        grid=(width // step_width,),
        in_specs=[SMEM] + [VMEM] * (5 + BLOCKS) + [by_head, by_head],
        out_specs=[by_head] + [VMEM] * (BLOCKS + 1),
        out_shape=[
            jax.ShapeDtypeStruct((rows, width), jnp.bfloat16),
            jax.ShapeDtypeStruct((rows, 2 * HD), jnp.float32),
            part, part, part, part,
            jax.ShapeDtypeStruct((fan, 2, HD), jnp.float32),
        ],
        scratch_shapes=[
            pltpu.VMEM((size, HD), jnp.bfloat16),
            pltpu.VMEM((size, HD), jnp.bfloat16),
            pltpu.VMEM((size, HD), jnp.float32),
            pltpu.VMEM((size, rows), jnp.float32),
            pltpu.VMEM((size, HD), jnp.float32),
            pltpu.VMEM((size, HD), jnp.float32),
            pltpu.VMEM((8, HD), jnp.float32),
        ],
        compiler_params=LIMIT,
        name="attention",
    )(scal, low, cos, sin, q_gain, k_gain, *window, queries, grads)


def finish(own, parts, kv, k_gain, cos, sin):
    rows = kv.shape[0]
    out = jax.ShapeDtypeStruct((rows, HD), jnp.bfloat16)
    return pl.pallas_call(
        functools.partial(final_kernel, rows),
        in_specs=[VMEM] * 9,
        out_specs=[VMEM, VMEM],
        out_shape=[out, out],
        compiler_params=LIMIT,
        name="finish",
    )(own, *parts, kv, k_gain, cos, sin)


CTX = ("y", "zh")
FAR = ("zl", "c", "zh", "x")


def shifted(block, distance):
    count = lax.axis_size("y") * lax.axis_size("zh")
    return lax.ppermute(block, CTX, [(i, (i + distance) % count) for i in range(count)])


def exchanged(copies, axes):
    return jnp.sum(lax.all_to_all(copies, axes, 0, 0), axis=0)


def on_device(queries_raw, keys_raw, values, grad_out, q_gain, k_gain, doc_lengths):
    rows = queries_raw.shape[1]
    fan = math.prod(lax.axis_size(a) for a in FAR)
    near = lax.axis_size("y")
    ctx_count = near * lax.axis_size("zh")
    shard = lax.axis_index("y") * lax.axis_size("zh") + lax.axis_index("zh")
    kv = jnp.concatenate([keys_raw[0], values[0]], axis=1)
    order = (4, 1, 3, 2)
    got = {d: shifted(kv, d) for d in order}
    first = (shard * rows).astype(jnp.int32).reshape(1)
    cos, sin, low, scal = prepare(doc_lengths, first, rows)
    q_gain2, k_gain2 = q_gain[None], k_gain[None]
    window = [kv] + [got[d] for d in range(1, BLOCKS)]
    dq, own, *terms, gains = attention(
        scal, low, cos, sin, q_gain2, k_gain2, window, queries_raw[0], grad_out[0], fan
    )
    back = {d: shifted(terms[d - 1], -d) for d in order}
    gains = exchanged(gains, FAR)
    gains = exchanged(jnp.broadcast_to(gains[None], (near,) + gains.shape), ("y",))
    loss_scale = (lax.axis_size("zl") * lax.axis_size("c") * ctx_count * rows) ** (-0.5)
    dk, dv = finish(own, [back[d] for d in range(1, BLOCKS)], kv, k_gain2, cos, sin)
    return (dq[None], dk[None], dv[None], gains * loss_scale)


def solution(mesh):
    fine = Mesh(mesh.devices.reshape(2, 2, 8, 4, 4), ("zl", "c", "y", "zh", "x"))
    split = P(("zl", "c"), ("y", "zh"), "x")
    return jax.shard_map(
        on_device,
        mesh=fine,
        in_specs=(split, split, split, split, P(), P(), P(("zl", "c"), None)),
        out_specs=(split, split, split, P()),
        check_vma=False,
    )
```

time: 275 us -> 92.8 us (0.34)
  the two profiles are of different devices: /device:TPU:1 before, /device:TPU:2 now
where the time goes in v1:
time: 92.8 us; the launch traced here: 92.2 us
  starting transfers between devices  63.3 us (68%)
  Pallas kernels  11.5 us (12%)
  waiting for transfers between devices  11 us (12%)
  local copies, waits for them, and re-layouts  4 us (4%)
  other arithmetic  1.64 us (2%)
    ppermute x8, starting transfers between devices, shifted(): lax.ppermute(block, CTX, [(i, (i + distance) % count) for i in range(coun...  42.1 us
    all_to_all x2, starting transfers between devices, exchanged(): return jnp.sum(lax.all_to_all(copies, axes, 0, 0), axis=0)  21.1 us
    pallas_call x1, Pallas kernels, attention(): pl.pallas_call(functools.partial(main_kernel, rows, fan), grid=(width //...  7.12 us
    all_to_all x2, waiting for transfers between devices, exchanged(): return jnp.sum(lax.all_to_all(copies, axes, 0, 0), axis=0)  6.82 us
    ppermute x8, waiting for transfers between devices, shifted(): lax.ppermute(block, CTX, [(i, (i + distance) % count) for i in range(coun...  4.13 us
    pallas_call x1, Pallas kernels, prepare(): pl.pallas_call(functools.partial(prep_kernel, rows, docs), in_specs=[SMEM...  3.52 us
    unnamed x14, local copies, waits for them, and re-layouts  3.4 us
  transfers between devices with their start and end apart: 10, of which 2 were waited for; matrix products, arithmetic and copies ran while one was open for 1% of the time, Pallas kernels for 5%

profile of v1, /device:TPU:2, one launch (start us, length us, event | category | flops | bytes accessed | tf_op | source)
XLA Modules:
  0.0 92.2 jit_solution(3379213404970711264)
XLA Ops:
  0.6 0.9 pad_maximum_fusion.w0.kv_ref
  1.5 3.5 %collective-permute-start.3 = (bf16[256,256]{1,0:T(8,128)(2,1)S(1)}, bf16[256,256]{1,0:T(8,128)(2,1)S(1)}, u32[]{:S(2)}, u32[]{:S(2)}) collective-permute-start(bf16[256,256]{1,0:T(8,128)(2,1)S(1)} %pad_maximum_fusion.w0.kv_ref), channel_id=1, source_target_pairs={{0,16},{4,20},{8,24},{12,28},{16,32},{20,36},{24,40},{28,44},{32,4... | collective-permute-start | bytes 393224 | tf_op jit(solution)/shard_map/ppermute | solution.py:262
  5.0 10.9 %collective-permute-start.2 = (bf16[256,256]{1,0:T(8,128)(2,1)S(1)}, bf16[256,256]{1,0:T(8,128)(2,1)S(1)}, u32[]{:S(2)}, u32[]{:S(2)}) collective-permute-start(bf16[256,256]{1,0:T(8,128)(2,1)S(1)} %pad_maximum_fusion.w0.kv_ref), channel_id=1, source_target_pairs={{0,12},{4,16},{8,20},{12,24},{16,28},{20,32},{24,36},{28,40},{32,4... | collective-permute-start | bytes 393224 | tf_op jit(solution)/shard_map/ppermute | solution.py:262
  16.0 1.9 %collective-permute-start.1 = (bf16[256,256]{1,0:T(8,128)(2,1)S(1)}, bf16[256,256]{1,0:T(8,128)(2,1)S(1)}, u32[]{:S(2)}, u32[]{:S(2)}) collective-permute-start(bf16[256,256]{1,0:T(8,128)(2,1)S(1)} %pad_maximum_fusion.w0.kv_ref), channel_id=1, source_target_pairs={{0,8},{4,12},{8,16},{12,20},{16,24},{20,28},{24,32},{28,36},{32,40... | collective-permute-start | bytes 393224 | tf_op jit(solution)/shard_map/ppermute | solution.py:262
  17.9 5.8 %collective-permute-start = (bf16[256,256]{1,0:T(8,128)(2,1)S(1)}, bf16[256,256]{1,0:T(8,128)(2,1)S(1)}, u32[]{:S(2)}, u32[]{:S(2)}) collective-permute-start(bf16[256,256]{1,0:T(8,128)(2,1)S(1)} %pad_maximum_fusion.w0.kv_ref), channel_id=1, source_target_pairs={{0,4},{4,8},{8,12},{12,16},{16,20},{20,24},{24,28},{28,32},{32,36}... | collective-permute-start | bytes 393224 | tf_op jit(solution)/shard_map/ppermute | solution.py:262
  23.7 0.1 maximum_bitcast_fusion.freq_ref
  23.8 0.0 copy-start.5
  23.8 0.7 copy-done.5
  24.5 0.0 copy-start
  24.5 1.0 %copy-done = f32[1024,128]{1,0:T(8,128)S(1)} copy-done((f32[1024,128]{1,0:T(8,128)S(1)}, f32[1024,128]{1,0:T(8,128)}, u32[]{:S(2)}) %copy-start) | copy-done | bytes 524312
  25.5 0.0 copy-start.1
  25.5 1.0 %copy-done.1 = f32[1024,128]{1,0:T(8,128)S(1)} copy-done((f32[1024,128]{1,0:T(8,128)S(1)}, f32[1024,128]{1,0:T(8,128)}, u32[]{:S(2)}) %copy-start.1) | copy-done | bytes 524312
  26.5 0.0 copy-start.2
  26.5 0.0 copy-start.3
  26.6 3.5 %prep.1 = (f32[1280,128]{1,0:T(8,128)S(1)}, f32[1280,128]{1,0:T(8,128)S(1)}, s32[8,256]{1,0:T(8,128)S(1)}, s32[2]{0:T(128)S(1)}) custom-call(s32[1,64]{1,0:T(1,128)S(1)} %copy-done.5, s32[1]{0:T(128)} %bitcast.first_ref, f32[1,128]{1,0:T(1,128)S(1)} %maximum_bitcast_fusion.freq_ref, f32[1024,128]{1,0:T(8,128)S(1)} %copy-done.1, f32[1024,128]{1,0:T(8,128)S(1)} %copy-done), custom_call_target="tpu_custom_call" | custom-call | tf_op jit(solution)/shard_map/prep/pallas_call | solution.py:197
  30.1 0.0 collective-permute-done.3.w4
  30.1 0.0 collective-permute-done.2.w3
  30.1 4.1 %collective-permute-done.1.w2 = bf16[256,256]{1,0:T(8,128)(2,1)S(1)} collective-permute-done((bf16[256,256]{1,0:T(8,128)(2,1)S(1)}, bf16[256,256]{1,0:T(8,128)(2,1)S(1)}, u32[]{:S(2)}, u32[]{:S(2)}) %collective-permute-start.1) | collective-permute-done | bytes 131104 | tf_op jit(solution)/shard_map/ppermute | solution.py:262
  34.2 0.0 collective-permute-done.w1
  34.2 0.0 copy-start.4
  34.2 0.0 copy-start.6
  34.2 0.0 copy-done.2
  34.2 0.0 copy-done.3
  34.2 0.6 copy-done.4
  34.9 0.0 copy-done.6
  34.9 7.1 %attention.1 = (bf16[256,1024]{1,0:T(8,128)(2,1)}, f32[256,256]{1,0:T(8,128)S(1)}, bf16[256,256]{1,0:T(8,128)(2,1)S(1)}, bf16[256,256]{1,0:T(8,128)(2,1)S(1)}, b...) custom-call(s32[2]{0:T(128)S(1)} %get-tuple-element.17.scal_ref, ...), custom_call_target="tpu_custom_call" | custom-call | tf_op jit(solution)/shard_map/attention/pallas_call | solution.py:218
  42.0 13.5 %all-to-all-start = ((f32[64,2,128]{2,1,0:T(2,128)}), f32[64,2,128]{2,1,0:T(2,128)S(1)}, u32[]{:S(2)}, u32[]{:S(2)}) async-start(f32[64,2,128]{2,1,0:T(2,128)} %get-tuple-element.29), calls=%async_computation | async-start | bytes 131072 | tf_op jit(solution)/shard_map/all_to_all | solution.py:266
  55.5 8.4 %collective-permute-start.4 = (bf16[256,256]{1,0:T(8,128)(2,1)S(1)}, bf16[256,256]{1,0:T(8,128)(2,1)S(1)}, u32[]{:S(2)}, u32[]{:S(2)}) collective-permute-start(bf16[256,256]{1,0:T(8,128)(2,1)S(1)} %get-tuple-element.23), channel_id=1, source_target_pairs={{0,124},{4,0},{8,4},{12,8},{16,12},{20,16},{24,20},{28,24},{32,28}... | collective-permute-start | bytes 393224 | tf_op jit(solution)/shard_map/ppermute | solution.py:262
  63.8 4.3 %collective-permute-start.5 = (bf16[256,256]{1,0:T(8,128)(2,1)S(1)}, bf16[256,256]{1,0:T(8,128)(2,1)S(1)}, u32[]{:S(2)}, u32[]{:S(2)}) collective-permute-start(bf16[256,256]{1,0:T(8,128)(2,1)S(1)} %get-tuple-element.24), channel_id=1, source_target_pairs={{0,120},{4,124},{8,0},{12,4},{16,8},{20,12},{24,16},{28,20},{32,24... | collective-permute-start | bytes 393224 | tf_op jit(solution)/shard_map/ppermute | solution.py:262
  68.1 5.4 %collective-permute-start.6 = (bf16[256,256]{1,0:T(8,128)(2,1)S(1)}, bf16[256,256]{1,0:T(8,128)(2,1)S(1)}, u32[]{:S(2)}, u32[]{:S(2)}) collective-permute-start(bf16[256,256]{1,0:T(8,128)(2,1)S(1)} %get-tuple-element.25), channel_id=1, source_target_pairs={{0,116},{4,120},{8,124},{12,0},{16,4},{20,8},{24,12},{28,16},{32,2... | collective-permute-start | bytes 393224 | tf_op jit(solution)/shard_map/ppermute | solution.py:262
  73.6 1.9 %collective-permute-start.7 = (bf16[256,256]{1,0:T(8,128)(2,1)S(1)}, bf16[256,256]{1,0:T(8,128)(2,1)S(1)}, u32[]{:S(2)}, u32[]{:S(2)}) collective-permute-start(bf16[256,256]{1,0:T(8,128)(2,1)S(1)} %get-tuple-element.26), channel_id=1, source_target_pairs={{0,112},{4,116},{8,120},{12,124},{16,0},{20,4},{24,8},{28,12},{32,... | collective-permute-start | bytes 393224 | tf_op jit(solution)/shard_map/ppermute | solution.py:262
  75.5 0.0 all-to-all-done
  75.5 0.1 reduce_sum.18
  75.6 0.6 broadcast_in_dim.30
  76.2 7.7 %all-to-all-start.1 = ((f32[8,2,128]{2,1,0:T(2,128)}), f32[8,2,128]{2,1,0:T(2,128)S(1)}, u32[]{:S(2)}, u32[]{:S(2)}) async-start(f32[8,2,128]{2,1,0:T(2,128)} %broadcast_in_dim.30), calls=%async_computation.1 | async-start | bytes 16384 | tf_op jit(solution)/shard_map/all_to_all | solution.py:266
  83.9 0.0 collective-permute-done.4.r1
  83.9 0.0 collective-permute-done.5.r2
  83.9 0.0 collective-permute-done.6.r3
  83.9 0.0 collective-permute-done.7.r4
  83.9 0.9 finish.1
  84.8 6.8 %all-to-all-done.1 = f32[8,2,128]{2,1,0:T(2,128)S(1)} async-done(((f32[8,2,128]{2,1,0:T(2,128)}), f32[8,2,128]{2,1,0:T(2,128)S(1)}, u32[]{:S(2)}, u32[]{:S(2)}) %all-to-all-start.1) | async-done | bytes 8224 | tf_op jit(solution)/shard_map/all_to_all | solution.py:266
  91.6 0.6 broadcast_multiply_fusion
  (2 shorter events, 0.0 us)
Async XLA Ops:
  1.5 28.6 %collective-permute-start.3 = (bf16[256,256]{1,0:T(8,128)(2,1)S(1)}, bf16[256,256]{1,0:T(8,128)(2,1)S(1)}, u32[]{:S(2)}, u32[]{:S(2)}) collective-permute-start(bf16[256,256]{1,0:T(8,128)(2,1)S(1)} %pad_maximum_fusion.w0.kv_ref), channel_id=1, source_target_pairs={{0,16},{4,20},{8,24},{12,28},{16,32},{20,36},{24,40},{28,44},{32,4... | collective-permute-start | bytes 393224 | tf_op jit(solution)/shard_map/ppermute | solution.py:262
  5.0 25.1 %collective-permute-start.2 = (bf16[256,256]{1,0:T(8,128)(2,1)S(1)}, bf16[256,256]{1,0:T(8,128)(2,1)S(1)}, u32[]{:S(2)}, u32[]{:S(2)}) collective-permute-start(bf16[256,256]{1,0:T(8,128)(2,1)S(1)} %pad_maximum_fusion.w0.kv_ref), channel_id=1, source_target_pairs={{0,12},{4,16},{8,20},{12,24},{16,28},{20,32},{24,36},{28,40},{32,4... | collective-permute-start | bytes 393224 | tf_op jit(solution)/shard_map/ppermute | solution.py:262
  16.0 18.2 %collective-permute-start.1 = (bf16[256,256]{1,0:T(8,128)(2,1)S(1)}, bf16[256,256]{1,0:T(8,128)(2,1)S(1)}, u32[]{:S(2)}, u32[]{:S(2)}) collective-permute-start(bf16[256,256]{1,0:T(8,128)(2,1)S(1)} %pad_maximum_fusion.w0.kv_ref), channel_id=1, source_target_pairs={{0,8},{4,12},{8,16},{12,20},{16,24},{20,28},{24,32},{28,36},{32,40... | collective-permute-start | bytes 393224 | tf_op jit(solution)/shard_map/ppermute | solution.py:262
  17.9 16.3 %collective-permute-start = (bf16[256,256]{1,0:T(8,128)(2,1)S(1)}, bf16[256,256]{1,0:T(8,128)(2,1)S(1)}, u32[]{:S(2)}, u32[]{:S(2)}) collective-permute-start(bf16[256,256]{1,0:T(8,128)(2,1)S(1)} %pad_maximum_fusion.w0.kv_ref), channel_id=1, source_target_pairs={{0,4},{4,8},{8,12},{12,16},{16,20},{20,24},{24,28},{28,32},{32,36}... | collective-permute-start | bytes 393224 | tf_op jit(solution)/shard_map/ppermute | solution.py:262
  23.8 0.7 copy-start.5
  24.5 1.0 %copy-start = (f32[1024,128]{1,0:T(8,128)S(1)}, f32[1024,128]{1,0:T(8,128)}, u32[]{:S(2)}) copy-start(f32[1024,128]{1,0:T(8,128)} %constant.26.clone.tabs_ref) | copy-start | bytes 1572868
  25.5 1.0 %copy-start.1 = (f32[1024,128]{1,0:T(8,128)S(1)}, f32[1024,128]{1,0:T(8,128)}, u32[]{:S(2)}) copy-start(f32[1024,128]{1,0:T(8,128)} %constant.25.clone.tabc_ref) | copy-start | bytes 1572868
  26.5 7.7 %copy-start.2 = (bf16[1,256,1024]{2,1,0:T(8,128)(2,1)S(1)}, bf16[1,256,1024]{2,1,0:T(8,128)(2,1)}, u32[]{:S(2)}) copy-start(bf16[1,256,1024]{2,1,0:T(8,128)(2,1)} %param.9) | copy-start | bytes 1572868
  26.5 7.7 %copy-start.3 = (bf16[1,256,1024]{2,1,0:T(8,128)(2,1)S(1)}, bf16[1,256,1024]{2,1,0:T(8,128)(2,1)}, u32[]{:S(2)}) copy-start(bf16[1,256,1024]{2,1,0:T(8,128)(2,1)} %param.12) | copy-start | bytes 1572868
  34.2 0.7 copy-start.4
  34.2 0.7 copy-start.6
  42.0 33.5 %all-to-all-start = ((f32[64,2,128]{2,1,0:T(2,128)}), f32[64,2,128]{2,1,0:T(2,128)S(1)}, u32[]{:S(2)}, u32[]{:S(2)}) async-start(f32[64,2,128]{2,1,0:T(2,128)} %get-tuple-element.29), calls=%async_computation | async-start | bytes 131072 | tf_op jit(solution)/shard_map/all_to_all | solution.py:266
  55.5 28.4 %collective-permute-start.4 = (bf16[256,256]{1,0:T(8,128)(2,1)S(1)}, bf16[256,256]{1,0:T(8,128)(2,1)S(1)}, u32[]{:S(2)}, u32[]{:S(2)}) collective-permute-start(bf16[256,256]{1,0:T(8,128)(2,1)S(1)} %get-tuple-element.23), channel_id=1, source_target_pairs={{0,124},{4,0},{8,4},{12,8},{16,12},{20,16},{24,20},{28,24},{32,28}... | collective-permute-start | bytes 393224 | tf_op jit(solution)/shard_map/ppermute | solution.py:262
  63.8 20.0 %collective-permute-start.5 = (bf16[256,256]{1,0:T(8,128)(2,1)S(1)}, bf16[256,256]{1,0:T(8,128)(2,1)S(1)}, u32[]{:S(2)}, u32[]{:S(2)}) collective-permute-start(bf16[256,256]{1,0:T(8,128)(2,1)S(1)} %get-tuple-element.24), channel_id=1, source_target_pairs={{0,120},{4,124},{8,0},{12,4},{16,8},{20,12},{24,16},{28,20},{32,24... | collective-permute-start | bytes 393224 | tf_op jit(solution)/shard_map/ppermute | solution.py:262
  68.1 15.8 %collective-permute-start.6 = (bf16[256,256]{1,0:T(8,128)(2,1)S(1)}, bf16[256,256]{1,0:T(8,128)(2,1)S(1)}, u32[]{:S(2)}, u32[]{:S(2)}) collective-permute-start(bf16[256,256]{1,0:T(8,128)(2,1)S(1)} %get-tuple-element.25), channel_id=1, source_target_pairs={{0,116},{4,120},{8,124},{12,0},{16,4},{20,8},{24,12},{28,16},{32,2... | collective-permute-start | bytes 393224 | tf_op jit(solution)/shard_map/ppermute | solution.py:262
  73.6 10.3 %collective-permute-start.7 = (bf16[256,256]{1,0:T(8,128)(2,1)S(1)}, bf16[256,256]{1,0:T(8,128)(2,1)S(1)}, u32[]{:S(2)}, u32[]{:S(2)}) collective-permute-start(bf16[256,256]{1,0:T(8,128)(2,1)S(1)} %get-tuple-element.26), channel_id=1, source_target_pairs={{0,112},{4,116},{8,120},{12,124},{16,0},{20,4},{24,8},{28,12},{32,... | collective-permute-start | bytes 393224 | tf_op jit(solution)/shard_map/ppermute | solution.py:262
  76.2 15.4 %all-to-all-start.1 = ((f32[8,2,128]{2,1,0:T(2,128)}), f32[8,2,128]{2,1,0:T(2,128)S(1)}, u32[]{:S(2)}, u32[]{:S(2)}) async-start(f32[8,2,128]{2,1,0:T(2,128)} %broadcast_in_dim.30), calls=%async_computation.1 | async-start | bytes 16384 | tf_op jit(solution)/shard_map/all_to_all | solution.py:266

commit v2 on v1

v2 whole, which is shorter than its diff:
```python
import functools
import math

import jax
import jax.numpy as jnp
from jax import lax
from jax.experimental import pallas as pl
from jax.experimental.pallas import tpu as pltpu
from jax.sharding import Mesh
from jax.sharding import PartitionSpec as P

REACH = 4
EPSILON = 1e-06
ROPE_BASE = 1000000.0
HD = 128
HALF = HD // 2
BLOCKS = REACH + 1
CHUNK = 128
GROUP = 2
UNROLL = 1
MASKED = -1e30
LOG2E = 1.4426950408889634
SCALE = HD ** (-0.5)
ACROSS = (((1,), (1,)), ((), ()))
ALONG = (((0,), (0,)), ((), ()))


def chunk_rows(i):
    return slice(i * CHUNK, (i + 1) * CHUNK)


def normed_of(source):
    values32 = source.astype(jnp.float32)
    inv = lax.rsqrt(jnp.mean(values32 * values32, axis=-1, keepdims=True) + EPSILON)
    return values32 * inv, inv


def rope(scaled, cos, sin):
    return scaled * cos + pltpu.roll(scaled, HALF, 1) * sin


def unrope(grad, cos, sin):
    return grad * cos - pltpu.roll(grad, HALF, 1) * sin


def fold(terms):
    return jnp.sum(terms.reshape(terms.shape[0] // 8, 8, terms.shape[1]), axis=0)


def fold_max(terms):
    return jnp.max(terms.reshape(terms.shape[0] // 8, 8, terms.shape[1]), axis=0)


def prep_kernel(
    rows, docs, first_ref, lens_ref, gains_ref, q_ref, kv_ref,
    cos_ref, sin_ref, bias_ref, qrot_ref, qnorm_ref, qinv_ref, krot_ref, knorm_ref, gain_ref, scal_ref,
):
    first = first_ref[0]
    chunks = rows // CHUNK
    heads = q_ref.shape[1] // HD
    tok_row = lax.broadcasted_iota(jnp.int32, (8, rows), 1)
    lane = lax.broadcasted_iota(jnp.int32, (8, HD), 1)
    row8 = lax.broadcasted_iota(jnp.int32, (8, HD), 0)
    sign = jnp.where(lane[0:1] < HALF, -1.0, 1.0).astype(jnp.float32)
    half_lane = jnp.where(lane < HALF, lane, lane - HALF).astype(jnp.float32)
    freq = jnp.exp(half_lane * (-2.0 * math.log(ROPE_BASE) / HD))[0:1]
    within = lax.broadcasted_iota(jnp.int32, (CHUNK, HD), 0).astype(jnp.float32) * freq
    within_c, within_s = jnp.cos(within), jnp.sin(within)

    def one_doc(d, carry):
        start, reaching, row = carry
        rel = start - first
        start = start + lens_ref[0, d]
        reaching = jnp.where(rel <= 0, rel, reaching)
        row = jnp.where(tok_row >= rel, rel, row)
        return start, reaching, row

    zero = jnp.int32(0)
    _, reaching, low = lax.fori_loop(0, docs, one_doc, (zero, zero, jnp.zeros((8, rows), jnp.int32)))
    before = -reaching
    scal_ref[0] = 1 + (before + rows - 1) // rows
    position = (tok_row - low).astype(jnp.float32)
    columns = [jnp.broadcast_to(position[0:1, chunk_rows(c)], (CHUNK, CHUNK)).T for c in range(chunks)]
    angles = jnp.where(lane[0:1] < HALF, columns[0], columns[1]) * freq
    packed_c, packed_s = jnp.cos(angles), jnp.sin(angles)
    rolled_c, rolled_s = pltpu.roll(packed_c, HALF, 1), pltpu.roll(packed_s, HALF, 1)
    low_lane = lane[0:1] < HALF
    cos = jnp.concatenate([jnp.where(low_lane, packed_c, rolled_c), jnp.where(low_lane, rolled_c, packed_c)], axis=0)
    sin = jnp.concatenate([jnp.where(low_lane, packed_s, rolled_s), jnp.where(low_lane, rolled_s, packed_s)], axis=0)
    sin = sin * sign
    cos_ref[0:rows, :] = cos
    sin_ref[0:rows, :] = sin
    base = (before - rows * (row8 // chunks + 1) + CHUNK * (row8 % chunks)).astype(jnp.float32) * freq
    base_c, base_s = jnp.cos(base), jnp.sin(base)
    for j in range(chunks * REACH):
        at = chunk_rows(chunks + j)
        c, s = base_c[j : j + 1], base_s[j : j + 1]
        cos_ref[at, :] = c * within_c - s * within_s
        sin_ref[at, :] = (s * within_c + c * within_s) * sign
    key = lax.broadcasted_iota(jnp.int32, (CHUNK, rows), 0)
    tok = lax.broadcasted_iota(jnp.int32, (CHUNK, rows), 1)
    for i in range(chunks + chunks * REACH):
        offset = i % chunks * CHUNK - i // chunks * rows
        kept = key + offset >= low[0:1, :]
        if i < chunks:
            kept = kept & (key + offset <= tok)
        bias_ref[chunk_rows(i), :] = jnp.where(kept, 0.0, MASKED)
    gain_ref[...] = gains_ref[...]
    q_gain, k_gain = gains_ref[0:1], gains_ref[1:2]
    normed, _ = normed_of(kv_ref[:, :HD])
    knorm_ref[...] = normed
    krot_ref[...] = rope(normed * k_gain, cos, sin).astype(jnp.bfloat16)
    for h in range(heads):
        normed, inv = normed_of(q_ref[:, h * HD : (h + 1) * HD])
        qnorm_ref[h] = normed
        qinv_ref[h] = jnp.broadcast_to(inv, (rows, HD))
        qrot_ref[h] = rope(normed * q_gain, cos, sin).astype(jnp.bfloat16)


def main_kernel(
    rows,
    scal_ref, cos_ref, sin_ref, bias_ref, qrot_ref, qnorm_ref, qinv_ref, krot0_ref, knorm0_ref,
    gain_ref, g_ref, w4, w1, w3, w2, w0,
    dq_ref, own_ref, o1, o2, o3, o4, sums_ref,
    krot, vwin, knorm, dk, dv, sums,
):
    heads = qrot_ref.shape[0]
    window = (w0, w1, w2, w3, w4)
    outs = (own_ref, o1, o2, o3, o4)
    q_gain, k_gain = gain_ref[0:1], gain_ref[1:2]
    count = scal_ref[0]
    sums[...] = jnp.zeros_like(sums)
    krot[0:rows, :] = krot0_ref[...]
    knorm[0:rows, :] = knorm0_ref[...]

    def block_rows(d):
        return slice(d * rows, (d + 1) * rows)

    def block_start(d):
        at = block_rows(d)
        vwin[at, :] = window[d][:, HD:]
        dk[at, :] = jnp.zeros((rows, HD), jnp.float32)
        dv[at, :] = jnp.zeros((rows, HD), jnp.float32)
        if d > 0:
            normed, _ = normed_of(window[d][:, :HD])
            knorm[at, :] = normed
            krot[at, :] = rope(normed * k_gain, cos_ref[at, :], sin_ref[at, :]).astype(jnp.bfloat16)

    block_start(0)
    for d in range(1, BLOCKS):
        pl.when(d < count)(functools.partial(block_start, d))

    def attend_group(first, blocks):
        q_rot = qrot_ref[pl.ds(first, GROUP)].reshape(GROUP * rows, HD)
        grad = jnp.concatenate(
            [g_ref[:, pl.ds(pl.multiple_of((first + i) * HD, HD), HD)] for i in range(GROUP)], axis=0
        )
        keys = [chunk_rows(i) for i in range(blocks * rows // CHUNK)]
        scores, wgrads, top = [], [], None
        for at in keys:
            mask = jnp.concatenate([bias_ref[at, :]] * GROUP, axis=1)
            part = lax.dot_general(krot[at, :], q_rot, ACROSS, preferred_element_type=jnp.float32) + mask
            scores.append(part)
            top = fold_max(part) if top is None else jnp.maximum(top, fold_max(part))
        top = jnp.max(top, axis=0, keepdims=True)
        powers, total, dot = [], 0.0, 0.0
        for at, part in zip(keys, scores):
            wgrad = lax.dot_general(vwin[at, :], grad, ACROSS, preferred_element_type=jnp.float32)
            power = jnp.exp2((part - top) * (SCALE * LOG2E))
            total = total + fold(power)
            dot = dot + fold(power * wgrad)
            powers.append(power)
            wgrads.append(wgrad)
        inv_sum = 1.0 / jnp.sum(total, axis=0, keepdims=True)
        delta = jnp.sum(dot, axis=0, keepdims=True) * inv_sum
        sgrads = []
        for at, power, wgrad in zip(keys, powers, wgrads):
            weights = power * inv_sum
            sgrad = (weights * (wgrad - delta)).astype(jnp.bfloat16)
            dv[at, :] += jnp.dot(weights.astype(jnp.bfloat16), grad, preferred_element_type=jnp.float32)
            dk[at, :] += jnp.dot(sgrad, q_rot, preferred_element_type=jnp.float32)
            sgrads.append(sgrad)
        q_grads = 0.0
        for at, sgrad in zip(keys, sgrads):
            q_grads = q_grads + lax.dot_general(sgrad, krot[at, :], ALONG, preferred_element_type=jnp.float32)
        cos, sin = cos_ref[0:rows, :], sin_ref[0:rows, :]
        for i in range(GROUP):
            h = first + i
            q_normed = qnorm_ref[h]
            norm_grad = unrope(q_grads[i * rows : (i + 1) * rows] * SCALE, cos, sin)
            sums[0:8, :] += fold(norm_grad * q_normed)
            gained = norm_grad * q_gain
            mean = jnp.mean(gained * q_normed, axis=-1, keepdims=True)
            dq_ref[:, pl.ds(pl.multiple_of(h * HD, HD), HD)] = ((gained - q_normed * mean) * qinv_ref[h]).astype(jnp.bfloat16)

    def attend(blocks):
        @pl.loop(0, heads // (GROUP * UNROLL))
        def _(j):
            for u in range(UNROLL):
                attend_group((j * UNROLL + u) * GROUP, blocks)

    for blocks in range(1, BLOCKS + 1):
        pl.when(count == blocks)(functools.partial(attend, blocks))

    def block_end(d):
        at = block_rows(d)
        key_grad = dk[at, :] * SCALE
        outs[d][:, :HD] = key_grad.astype(outs[d].dtype)
        outs[d][:, HD:] = dv[at, :].astype(outs[d].dtype)
        norm_grad = unrope(key_grad, cos_ref[at, :], sin_ref[at, :])
        sums[8:16, :] += fold(norm_grad * knorm[at, :])

    def block_unused(d):
        outs[d][...] = jnp.zeros_like(outs[d])

    block_end(0)
    for d in range(1, BLOCKS):
        pl.when(d < count)(functools.partial(block_end, d))
        pl.when(d >= count)(functools.partial(block_unused, d))
    q_sum = jnp.sum(sums[0:8, :], axis=0, keepdims=True)
    k_sum = jnp.sum(sums[8:16, :], axis=0, keepdims=True)
    both = jnp.concatenate([q_sum, k_sum], axis=0)
    sums_ref[...] = jnp.broadcast_to(both[None], sums_ref.shape)


def final_kernel(rows, own_ref, r1, r2, r3, r4, kv_ref, gain_ref, cos_ref, sin_ref, dk_ref, dv_ref):
    total = own_ref[...]
    for part in (r1, r2, r3, r4):
        total = total + part[...].astype(jnp.float32)
    dv_ref[...] = total[:, HD:].astype(jnp.bfloat16)
    normed, inv = normed_of(kv_ref[:, :HD])
    gained = unrope(total[:, :HD], cos_ref[0:rows, :], sin_ref[0:rows, :]) * gain_ref[1:2]
    mean = jnp.mean(gained * normed, axis=-1, keepdims=True)
    dk_ref[...] = ((gained - normed * mean) * inv).astype(jnp.bfloat16)


VMEM = pl.BlockSpec(memory_space=pltpu.VMEM)
SMEM = pl.BlockSpec(memory_space=pltpu.SMEM)
F32 = functools.partial(jax.ShapeDtypeStruct, dtype=jnp.float32)
BF16 = functools.partial(jax.ShapeDtypeStruct, dtype=jnp.bfloat16)
I32 = functools.partial(jax.ShapeDtypeStruct, dtype=jnp.int32)


def limit(mib):
    return pltpu.CompilerParams(vmem_limit_bytes=mib * 1024 * 1024)


def prepare(doc_lengths, first, gains, queries, kv):
    docs = doc_lengths.shape[1]
    rows, width = queries.shape
    heads = width // HD
    size = BLOCKS * rows
    return pl.pallas_call(
        functools.partial(prep_kernel, rows, docs),
        in_specs=[SMEM, SMEM] + [VMEM] * 3,
        out_specs=[VMEM] * 9 + [SMEM],
        out_shape=[
            F32((size, HD)), F32((size, HD)), F32((size, rows)),
            BF16((heads, rows, HD)), F32((heads, rows, HD)), F32((heads, rows, HD)),
            BF16((rows, HD)), F32((rows, HD)), F32((2, HD)),
            I32((1,)),
        ],
        compiler_params=limit(24),
        name="prep",
    )(first, doc_lengths, gains, queries, kv)


def attention(prepared, grads, window, fan):
    *tables, scal = prepared
    rows, width = grads.shape
    size = BLOCKS * rows
    return pl.pallas_call(
        functools.partial(main_kernel, rows),
        in_specs=[SMEM] + [VMEM] * (len(tables) + 1 + BLOCKS),
        out_specs=[VMEM] * (BLOCKS + 2),
        out_shape=[BF16((rows, width)), F32((rows, 2 * HD))] + [BF16((rows, 2 * HD))] * REACH + [F32((fan, 2, HD))],
        scratch_shapes=[
            pltpu.VMEM((size, HD), jnp.bfloat16),
            pltpu.VMEM((size, HD), jnp.bfloat16),
            pltpu.VMEM((size, HD), jnp.float32),
            pltpu.VMEM((size, HD), jnp.float32),
            pltpu.VMEM((size, HD), jnp.float32),
            pltpu.VMEM((16, HD), jnp.float32),
        ],
        compiler_params=limit(32),
        name="attention",
    )(scal, *tables, grads, window[4], window[1], window[3], window[2], window[0])


def finish(own, parts, kv, prepared):
    rows = kv.shape[0]
    return pl.pallas_call(
        functools.partial(final_kernel, rows),
        in_specs=[VMEM] * 9,
        out_specs=[VMEM, VMEM],
        out_shape=[BF16((rows, HD)), BF16((rows, HD))],
        compiler_params=limit(16),
        name="finish",
    )(own, *parts, kv, prepared[8], prepared[0], prepared[1])


CTX = ("y", "zh")
FAR = ("zl", "c", "zh", "x")


def shifted(block, distance):
    count = lax.axis_size("y") * lax.axis_size("zh")
    return lax.ppermute(block, CTX, [(i, (i + distance) % count) for i in range(count)])


def exchanged(copies, axes):
    return jnp.sum(lax.all_to_all(copies, axes, 0, 0), axis=0)


def on_device(queries_raw, keys_raw, values, grad_out, q_gain, k_gain, doc_lengths):
    rows = queries_raw.shape[1]
    fan = math.prod(lax.axis_size(a) for a in FAR)
    near = lax.axis_size("y")
    ctx_count = near * lax.axis_size("zh")
    shard = lax.axis_index("y") * lax.axis_size("zh") + lax.axis_index("zh")
    kv = jnp.concatenate([keys_raw[0], values[0]], axis=1)
    got = {d: shifted(kv, d) for d in (2, 3, 1, 4)}
    first = (shard * rows).astype(jnp.int32).reshape(1)
    prepared = prepare(doc_lengths, first, jnp.stack([q_gain, k_gain]), queries_raw[0], kv)
    window = [kv] + [got[d] for d in range(1, BLOCKS)]
    dq, own, *terms, gains = attention(prepared, grad_out[0], window, fan)
    back = {d: shifted(terms[d - 1], -d) for d in (2, 3, 1, 4)}
    gains = exchanged(gains, FAR)
    gains = exchanged(jnp.broadcast_to(gains[None], (near,) + gains.shape), ("y",))
    loss_scale = (lax.axis_size("zl") * lax.axis_size("c") * ctx_count * rows) ** (-0.5)
    dk, dv = finish(own, [back[d] for d in range(1, BLOCKS)], kv, prepared)
    return (dq[None], dk[None], dv[None], gains * loss_scale)


def solution(mesh):
    fine = Mesh(mesh.devices.reshape(2, 2, 8, 4, 4), ("zl", "c", "y", "zh", "x"))
    split = P(("zl", "c"), ("y", "zh"), "x")
    return jax.shard_map(
        on_device,
        mesh=fine,
        in_specs=(split, split, split, split, P(), P(), P(("zl", "c"), None)),
        out_specs=(split, split, split, P()),
        check_vma=False,
    )
```

time: 92.8 us -> 84.4 us (0.909)
  waiting for transfers between devices: 11 us -> 6.87 us
  Pallas kernels: 11.5 us -> 9.54 us
  local copies, waits for them, and re-layouts: 4 us -> 2.3 us
  starting transfers between devices: 63.3 us -> 62.1 us
    all_to_all x2, starting transfers between devices: 21.1 us -> 16.2 us  [exchanged(): return jnp.sum(lax.all_to_all(copies, axes, 0, 0), axis=0)]
    ppermute x8, starting transfers between devices: 42.1 us -> 46 us  [shifted(): lax.ppermute(block, CTX, [(i, (i + distance) % count) for i in range(coun...]
    ppermute x8, waiting for transfers between devices: 4.13 us -> 0.88 us  [shifted(): lax.ppermute(block, CTX, [(i, (i + distance) % count) for i in range(coun...]
    unnamed x14 -> x6, local copies, waits for them, and re-layouts: 3.4 us -> 1.7 us
    pallas_call x1, Pallas kernels: 7.12 us -> 5.45 us  [attention(): pl.pallas_call(functools.partial(main_kernel, rows), in_specs=[SMEM] + [V...]
  transfers between devices with their start and end apart: 10 -> 10, of which waited for: 2 -> 2; matrix products, arithmetic and copies ran while one was open for 1% -> 2% of each run, Pallas kernels for 5% -> 5%
where the time goes in v2:
time: 84.4 us; the launch traced here: 83.9 us
  starting transfers between devices  62.1 us (74%)
  Pallas kernels  9.54 us (11%)
  waiting for transfers between devices  6.87 us (8%)
  local copies, waits for them, and re-layouts  2.3 us (3%)
  other arithmetic  2.29 us (3%)
    ppermute x8, starting transfers between devices, shifted(): lax.ppermute(block, CTX, [(i, (i + distance) % count) for i in range(coun...  46 us
    all_to_all x2, starting transfers between devices, exchanged(): return jnp.sum(lax.all_to_all(copies, axes, 0, 0), axis=0)  16.2 us
    all_to_all x2, waiting for transfers between devices, exchanged(): return jnp.sum(lax.all_to_all(copies, axes, 0, 0), axis=0)  5.99 us
    pallas_call x1, Pallas kernels, attention(): pl.pallas_call(functools.partial(main_kernel, rows), in_specs=[SMEM] + [V...  5.45 us
    pallas_call x1, Pallas kernels, prepare(): pl.pallas_call(functools.partial(prep_kernel, rows, docs), in_specs=[SMEM...  3.22 us
    unnamed x6, local copies, waits for them, and re-layouts  1.7 us
  transfers between devices with their start and end apart: 10, of which 2 were waited for; matrix products, arithmetic and copies ran while one was open for 2% of the time, Pallas kernels for 5%

profile of v2, /device:TPU:2, one launch (start us, length us, event | category | flops | bytes accessed | tf_op | source)
XLA Modules:
  0.0 83.9 jit_solution(9895627732744141250)
XLA Ops:
  0.6 0.0 copy-start
  0.6 0.9 %pad_maximum_fusion.kv_ref.w0 = bf16[256,256]{1,0:T(8,128)(2,1)S(1)} fusion(bf16[256,128]{1,0:T(8,128)(2,1)} %bitcast.12, bf16[256,128]{1,0:T(8,128)(2,1)} %bitcast.13), kind=kLoop, calls=%fused_computation | loop fusion | flops 262144 | bytes 262144 | tf_op jit(solution)/shard_map/concatenate | solution.py:321
  1.6 10.9 %collective-permute-start.3 = (bf16[256,256]{1,0:T(8,128)(2,1)S(1)}, bf16[256,256]{1,0:T(8,128)(2,1)S(1)}, u32[]{:S(2)}, u32[]{:S(2)}) collective-permute-start(bf16[256,256]{1,0:T(8,128)(2,1)S(1)} %pad_maximum_fusion.kv_ref.w0), channel_id=1, source_target_pairs={{0,8},{4,12},{8,16},{12,20},{16,24},{20,28},{24,32},{28,36},{32,40... | collective-permute-start | bytes 393224 | tf_op jit(solution)/shard_map/ppermute | solution.py:308
  12.5 1.9 %collective-permute-start.2 = (bf16[256,256]{1,0:T(8,128)(2,1)S(1)}, bf16[256,256]{1,0:T(8,128)(2,1)S(1)}, u32[]{:S(2)}, u32[]{:S(2)}) collective-permute-start(bf16[256,256]{1,0:T(8,128)(2,1)S(1)} %pad_maximum_fusion.kv_ref.w0), channel_id=1, source_target_pairs={{0,12},{4,16},{8,20},{12,24},{16,28},{20,32},{24,36},{28,40},{32,4... | collective-permute-start | bytes 393224 | tf_op jit(solution)/shard_map/ppermute | solution.py:308
  14.5 5.8 %collective-permute-start.1 = (bf16[256,256]{1,0:T(8,128)(2,1)S(1)}, bf16[256,256]{1,0:T(8,128)(2,1)S(1)}, u32[]{:S(2)}, u32[]{:S(2)}) collective-permute-start(bf16[256,256]{1,0:T(8,128)(2,1)S(1)} %pad_maximum_fusion.kv_ref.w0), channel_id=1, source_target_pairs={{0,4},{4,8},{8,12},{12,16},{16,20},{20,24},{24,28},{28,32},{32,36}... | collective-permute-start | bytes 393224 | tf_op jit(solution)/shard_map/ppermute | solution.py:308
  20.3 3.5 %collective-permute-start = (bf16[256,256]{1,0:T(8,128)(2,1)S(1)}, bf16[256,256]{1,0:T(8,128)(2,1)S(1)}, u32[]{:S(2)}, u32[]{:S(2)}) collective-permute-start(bf16[256,256]{1,0:T(8,128)(2,1)S(1)} %pad_maximum_fusion.kv_ref.w0), channel_id=1, source_target_pairs={{0,16},{4,20},{8,24},{12,28},{16,32},{20,36},{24,40},{28,44},{32,4... | collective-permute-start | bytes 393224 | tf_op jit(solution)/shard_map/ppermute | solution.py:308
  23.8 0.7 pad_maximum_fusion.1.gains_ref
  24.5 0.0 copy-start.1
  24.5 1.0 %copy-done.1 = bf16[1,256,1024]{2,1,0:T(8,128)(2,1)S(1)} copy-done((bf16[1,256,1024]{2,1,0:T(8,128)(2,1)S(1)}, bf16[1,256,1024]{2,1,0:T(8,128)(2,1)}, u32[]{:S(2)}) %copy-start.1) | copy-done | bytes 524312
  25.5 0.0 copy-start.2
  25.5 0.7 copy-done.2
  26.2 3.2 %prep.1 = (f32[1280,128]{1,0:T(8,128)S(1)}, f32[1280,128]{1,0:T(8,128)S(1)}, f32[1280,256]{1,0:T(8,128)S(1)}, bf16[8,256,128]{2,1,0:T(8,128)(2,1)S(1)}, f32[8,25...) custom-call(s32[1]{0:T(128)} %bitcast.first_ref, ...), custom_call_target="tpu_custom_call" | custom-call | tf_op jit(solution)/shard_map/prep/pallas_call | solution.py:253
  29.4 0.0 collective-permute-done.3.w2
  29.4 0.0 collective-permute-done.2.w3
  29.4 0.0 collective-permute-done.1.w1
  29.4 0.0 collective-permute-done.w4
  29.4 0.0 copy-done
  29.4 5.5 %attention.1 = (bf16[256,1024]{1,0:T(8,128)(2,1)}, f32[256,256]{1,0:T(8,128)S(1)}, bf16[256,256]{1,0:T(8,128)(2,1)S(1)}, bf16[256,256]{1,0:T(8,128)(2,1)S(1)}, b...) custom-call(s32[1]{0:T(128)} %get-tuple-element.23.scal_ref, ...), custom_call_target="tpu_custom_call" | custom-call | tf_op jit(solution)/shard_map/attention/pallas_call | solution.py:272
  34.9 11.3 %all-to-all-start = ((f32[64,2,128]{2,1,0:T(2,128)}), f32[64,2,128]{2,1,0:T(2,128)S(1)}, u32[]{:S(2)}, u32[]{:S(2)}) async-start(f32[64,2,128]{2,1,0:T(2,128)} %get-tuple-element.41), calls=%async_computation | async-start | bytes 131072 | tf_op jit(solution)/shard_map/all_to_all | solution.py:312
  46.2 10.8 %collective-permute-start.4 = (bf16[256,256]{1,0:T(8,128)(2,1)S(1)}, bf16[256,256]{1,0:T(8,128)(2,1)S(1)}, u32[]{:S(2)}, u32[]{:S(2)}) collective-permute-start(bf16[256,256]{1,0:T(8,128)(2,1)S(1)} %get-tuple-element.35), channel_id=1, source_target_pairs={{0,124},{4,0},{8,4},{12,8},{16,12},{20,16},{24,20},{28,24},{32,28}... | collective-permute-start | bytes 393224 | tf_op jit(solution)/shard_map/ppermute | solution.py:308
  57.1 4.3 %collective-permute-start.5 = (bf16[256,256]{1,0:T(8,128)(2,1)S(1)}, bf16[256,256]{1,0:T(8,128)(2,1)S(1)}, u32[]{:S(2)}, u32[]{:S(2)}) collective-permute-start(bf16[256,256]{1,0:T(8,128)(2,1)S(1)} %get-tuple-element.36), channel_id=1, source_target_pairs={{0,120},{4,124},{8,0},{12,4},{16,8},{20,12},{24,16},{28,20},{32,24... | collective-permute-start | bytes 393224 | tf_op jit(solution)/shard_map/ppermute | solution.py:308
  61.3 4.7 %collective-permute-start.6 = (bf16[256,256]{1,0:T(8,128)(2,1)S(1)}, bf16[256,256]{1,0:T(8,128)(2,1)S(1)}, u32[]{:S(2)}, u32[]{:S(2)}) collective-permute-start(bf16[256,256]{1,0:T(8,128)(2,1)S(1)} %get-tuple-element.37), channel_id=1, source_target_pairs={{0,116},{4,120},{8,124},{12,0},{16,4},{20,8},{24,12},{28,16},{32,2... | collective-permute-start | bytes 393224 | tf_op jit(solution)/shard_map/ppermute | solution.py:308
  66.1 4.0 %collective-permute-start.7 = (bf16[256,256]{1,0:T(8,128)(2,1)S(1)}, bf16[256,256]{1,0:T(8,128)(2,1)S(1)}, u32[]{:S(2)}, u32[]{:S(2)}) collective-permute-start(bf16[256,256]{1,0:T(8,128)(2,1)S(1)} %get-tuple-element.38), channel_id=1, source_target_pairs={{0,112},{4,116},{8,120},{12,124},{16,0},{20,4},{24,8},{28,12},{32,... | collective-permute-start | bytes 393224 | tf_op jit(solution)/shard_map/ppermute | solution.py:308
  70.1 0.0 all-to-all-done
  70.1 0.1 reduce_sum.18
  70.2 0.6 broadcast_in_dim.18
  70.8 4.9 %all-to-all-start.1 = ((f32[8,2,128]{2,1,0:T(2,128)}), f32[8,2,128]{2,1,0:T(2,128)S(1)}, u32[]{:S(2)}, u32[]{:S(2)}) async-start(f32[8,2,128]{2,1,0:T(2,128)} %broadcast_in_dim.18), calls=%async_computation.1 | async-start | bytes 16384 | tf_op jit(solution)/shard_map/all_to_all | solution.py:312
  75.6 0.0 collective-permute-done.4.r1
  75.6 0.9 %collective-permute-done.5.r2 = bf16[256,256]{1,0:T(8,128)(2,1)S(1)} collective-permute-done((bf16[256,256]{1,0:T(8,128)(2,1)S(1)}, bf16[256,256]{1,0:T(8,128)(2,1)S(1)}, u32[]{:S(2)}, u32[]{:S(2)}) %collective-permute-start.5) | collective-permute-done | bytes 131104 | tf_op jit(solution)/shard_map/ppermute | solution.py:308
  76.5 0.0 collective-permute-done.6.r3
  76.5 0.0 collective-permute-done.7.r4
  76.5 0.9 %finish.1 = (bf16[256,128]{1,0:T(8,128)(2,1)}, bf16[256,128]{1,0:T(8,128)(2,1)}) custom-call(f32[256,256]{1,0:T(8,128)S(1)} %get-tuple-element.34.own_ref, bf16[256,256]{1,0:T(8,128)(2,1)S(1)} %collective-permute-done.4.r1, bf16[256,256]{1,0:T(8,128)(2,1)S(1)} %collective-permute-done.5.r2, bf16[256,256]{1,0:T(8,128)(2,1)S(1)} %collective-permute-done.6.r3, ...), custom_call_target="tpu_custom_call" | custom-call | tf_op jit(solution)/shard_map/finish/pallas_call | solution.py:292
  77.4 6.0 %all-to-all-done.1 = f32[8,2,128]{2,1,0:T(2,128)S(1)} async-done(((f32[8,2,128]{2,1,0:T(2,128)}), f32[8,2,128]{2,1,0:T(2,128)S(1)}, u32[]{:S(2)}, u32[]{:S(2)}) %all-to-all-start.1) | async-done | bytes 8224 | tf_op jit(solution)/shard_map/all_to_all | solution.py:312
  83.4 0.6 broadcast_multiply_fusion
  (1 shorter events, 0.0 us)
Async XLA Ops:
  0.6 28.8 %copy-start = (bf16[1,256,1024]{2,1,0:T(8,128)(2,1)S(1)}, bf16[1,256,1024]{2,1,0:T(8,128)(2,1)}, u32[]{:S(2)}) copy-start(bf16[1,256,1024]{2,1,0:T(8,128)(2,1)} %param.10) | copy-start | bytes 1572868
  1.6 27.8 %collective-permute-start.3 = (bf16[256,256]{1,0:T(8,128)(2,1)S(1)}, bf16[256,256]{1,0:T(8,128)(2,1)S(1)}, u32[]{:S(2)}, u32[]{:S(2)}) collective-permute-start(bf16[256,256]{1,0:T(8,128)(2,1)S(1)} %pad_maximum_fusion.kv_ref.w0), channel_id=1, source_target_pairs={{0,8},{4,12},{8,16},{12,20},{16,24},{20,28},{24,32},{28,36},{32,40... | collective-permute-start | bytes 393224 | tf_op jit(solution)/shard_map/ppermute | solution.py:308
  12.5 16.9 %collective-permute-start.2 = (bf16[256,256]{1,0:T(8,128)(2,1)S(1)}, bf16[256,256]{1,0:T(8,128)(2,1)S(1)}, u32[]{:S(2)}, u32[]{:S(2)}) collective-permute-start(bf16[256,256]{1,0:T(8,128)(2,1)S(1)} %pad_maximum_fusion.kv_ref.w0), channel_id=1, source_target_pairs={{0,12},{4,16},{8,20},{12,24},{16,28},{20,32},{24,36},{28,40},{32,4... | collective-permute-start | bytes 393224 | tf_op jit(solution)/shard_map/ppermute | solution.py:308
  14.5 15.0 %collective-permute-start.1 = (bf16[256,256]{1,0:T(8,128)(2,1)S(1)}, bf16[256,256]{1,0:T(8,128)(2,1)S(1)}, u32[]{:S(2)}, u32[]{:S(2)}) collective-permute-start(bf16[256,256]{1,0:T(8,128)(2,1)S(1)} %pad_maximum_fusion.kv_ref.w0), channel_id=1, source_target_pairs={{0,4},{4,8},{8,12},{12,16},{16,20},{20,24},{24,28},{28,32},{32,36}... | collective-permute-start | bytes 393224 | tf_op jit(solution)/shard_map/ppermute | solution.py:308
  20.3 9.1 %collective-permute-start = (bf16[256,256]{1,0:T(8,128)(2,1)S(1)}, bf16[256,256]{1,0:T(8,128)(2,1)S(1)}, u32[]{:S(2)}, u32[]{:S(2)}) collective-permute-start(bf16[256,256]{1,0:T(8,128)(2,1)S(1)} %pad_maximum_fusion.kv_ref.w0), channel_id=1, source_target_pairs={{0,16},{4,20},{8,24},{12,28},{16,32},{20,36},{24,40},{28,44},{32,4... | collective-permute-start | bytes 393224 | tf_op jit(solution)/shard_map/ppermute | solution.py:308
  24.5 1.0 %copy-start.1 = (bf16[1,256,1024]{2,1,0:T(8,128)(2,1)S(1)}, bf16[1,256,1024]{2,1,0:T(8,128)(2,1)}, u32[]{:S(2)}) copy-start(bf16[1,256,1024]{2,1,0:T(8,128)(2,1)} %param.7) | copy-start | bytes 1572868
  25.5 0.7 copy-start.2
  34.9 35.2 %all-to-all-start = ((f32[64,2,128]{2,1,0:T(2,128)}), f32[64,2,128]{2,1,0:T(2,128)S(1)}, u32[]{:S(2)}, u32[]{:S(2)}) async-start(f32[64,2,128]{2,1,0:T(2,128)} %get-tuple-element.41), calls=%async_computation | async-start | bytes 131072 | tf_op jit(solution)/shard_map/all_to_all | solution.py:312
  46.2 29.4 %collective-permute-start.4 = (bf16[256,256]{1,0:T(8,128)(2,1)S(1)}, bf16[256,256]{1,0:T(8,128)(2,1)S(1)}, u32[]{:S(2)}, u32[]{:S(2)}) collective-permute-start(bf16[256,256]{1,0:T(8,128)(2,1)S(1)} %get-tuple-element.35), channel_id=1, source_target_pairs={{0,124},{4,0},{8,4},{12,8},{16,12},{20,16},{24,20},{28,24},{32,28}... | collective-permute-start | bytes 393224 | tf_op jit(solution)/shard_map/ppermute | solution.py:308
  57.1 19.4 %collective-permute-start.5 = (bf16[256,256]{1,0:T(8,128)(2,1)S(1)}, bf16[256,256]{1,0:T(8,128)(2,1)S(1)}, u32[]{:S(2)}, u32[]{:S(2)}) collective-permute-start(bf16[256,256]{1,0:T(8,128)(2,1)S(1)} %get-tuple-element.36), channel_id=1, source_target_pairs={{0,120},{4,124},{8,0},{12,4},{16,8},{20,12},{24,16},{28,20},{32,24... | collective-permute-start | bytes 393224 | tf_op jit(solution)/shard_map/ppermute | solution.py:308
  61.3 15.2 %collective-permute-start.6 = (bf16[256,256]{1,0:T(8,128)(2,1)S(1)}, bf16[256,256]{1,0:T(8,128)(2,1)S(1)}, u32[]{:S(2)}, u32[]{:S(2)}) collective-permute-start(bf16[256,256]{1,0:T(8,128)(2,1)S(1)} %get-tuple-element.37), channel_id=1, source_target_pairs={{0,116},{4,120},{8,124},{12,0},{16,4},{20,8},{24,12},{28,16},{32,2... | collective-permute-start | bytes 393224 | tf_op jit(solution)/shard_map/ppermute | solution.py:308
  66.1 10.4 %collective-permute-start.7 = (bf16[256,256]{1,0:T(8,128)(2,1)S(1)}, bf16[256,256]{1,0:T(8,128)(2,1)S(1)}, u32[]{:S(2)}, u32[]{:S(2)}) collective-permute-start(bf16[256,256]{1,0:T(8,128)(2,1)S(1)} %get-tuple-element.38), channel_id=1, source_target_pairs={{0,112},{4,116},{8,120},{12,124},{16,0},{20,4},{24,8},{28,12},{32,... | collective-permute-start | bytes 393224 | tf_op jit(solution)/shard_map/ppermute | solution.py:308
  70.8 12.6 %all-to-all-start.1 = ((f32[8,2,128]{2,1,0:T(2,128)}), f32[8,2,128]{2,1,0:T(2,128)S(1)}, u32[]{:S(2)}, u32[]{:S(2)}) async-start(f32[8,2,128]{2,1,0:T(2,128)} %broadcast_in_dim.18), calls=%async_computation.1 | async-start | bytes 16384 | tf_op jit(solution)/shard_map/all_to_all | solution.py:312

commit v3 on v2

--- a/solution.py
+++ b/solution.py
@@ -17,7 +17,8 @@
 BLOCKS = REACH + 1
 CHUNK = 128
 GROUP = 2
-UNROLL = 1
+UNROLL = 2
+LAG = 1
 MASKED = -1e30
 LOG2E = 1.4426950408889634
 SCALE = HD ** (-0.5)
@@ -162,6 +163,7 @@
             part = lax.dot_general(krot[at, :], q_rot, ACROSS, preferred_element_type=jnp.float32) + mask
             scores.append(part)
             top = fold_max(part) if top is None else jnp.maximum(top, fold_max(part))
+            yield
         top = jnp.max(top, axis=0, keepdims=True)
         powers, total, dot = [], 0.0, 0.0
         for at, part in zip(keys, scores):
@@ -171,6 +173,7 @@
             dot = dot + fold(power * wgrad)
             powers.append(power)
             wgrads.append(wgrad)
+            yield
         inv_sum = 1.0 / jnp.sum(total, axis=0, keepdims=True)
         delta = jnp.sum(dot, axis=0, keepdims=True) * inv_sum
         sgrads = []
@@ -180,9 +183,11 @@
             dv[at, :] += jnp.dot(weights.astype(jnp.bfloat16), grad, preferred_element_type=jnp.float32)
             dk[at, :] += jnp.dot(sgrad, q_rot, preferred_element_type=jnp.float32)
             sgrads.append(sgrad)
+            yield
         q_grads = 0.0
         for at, sgrad in zip(keys, sgrads):
             q_grads = q_grads + lax.dot_general(sgrad, krot[at, :], ALONG, preferred_element_type=jnp.float32)
+        yield
         cos, sin = cos_ref[0:rows, :], sin_ref[0:rows, :]
         for i in range(GROUP):
             h = first + i
@@ -196,8 +201,16 @@
     def attend(blocks):
         @pl.loop(0, heads // (GROUP * UNROLL))
         def _(j):
-            for u in range(UNROLL):
-                attend_group((j * UNROLL + u) * GROUP, blocks)
+            waiting = [attend_group((j * UNROLL + u) * GROUP, blocks) for u in range(UNROLL)]
+            running, tick = [], 0
+            lag = max(1, LAG * blocks * rows // CHUNK)
+            while waiting or running:
+                if waiting and tick % lag == 0:
+                    running.append(waiting.pop(0))
+                tick += 1
+                for group in list(running):
+                    if next(group, "end") == "end":
+                        running.remove(group)
 
     for blocks in range(1, BLOCKS + 1):
         pl.when(count == blocks)(functools.partial(attend, blocks))

time: 84.4 us -> 83.2 us (0.986)
    all_to_all x2, starting transfers between devices: 16.2 us -> 14.7 us  [exchanged(): return jnp.sum(lax.all_to_all(copies, axes, 0, 0), axis=0)]
    ppermute x8, starting transfers between devices: 46 us -> 46.9 us  [shifted(): lax.ppermute(block, CTX, [(i, (i + distance) % count) for i in range(coun...]
where the time goes in v3:
time: 83.2 us; the launch traced here: 82.7 us
  starting transfers between devices  61.7 us (74%)
  Pallas kernels  8.87 us (11%)
  waiting for transfers between devices  6.81 us (8%)
  local copies, waits for them, and re-layouts  2.3 us (3%)
  other arithmetic  2.29 us (3%)
    ppermute x8, starting transfers between devices, shifted(): lax.ppermute(block, CTX, [(i, (i + distance) % count) for i in range(coun...  46.9 us
    all_to_all x2, starting transfers between devices, exchanged(): return jnp.sum(lax.all_to_all(copies, axes, 0, 0), axis=0)  14.7 us
    all_to_all x2, waiting for transfers between devices, exchanged(): return jnp.sum(lax.all_to_all(copies, axes, 0, 0), axis=0)  5.98 us
    pallas_call x1, Pallas kernels, attention(): pl.pallas_call(functools.partial(main_kernel, rows), in_specs=[SMEM] + [V...  4.79 us
    pallas_call x1, Pallas kernels, prepare(): pl.pallas_call(functools.partial(prep_kernel, rows, docs), in_specs=[SMEM...  3.22 us
    unnamed x6, local copies, waits for them, and re-layouts  1.7 us
  transfers between devices with their start and end apart: 10, of which 2 were waited for; matrix products, arithmetic and copies ran while one was open for 2% of the time, Pallas kernels for 5%

profile of v3, /device:TPU:2, one launch (start us, length us, event | category | flops | bytes accessed | tf_op | source)
XLA Modules:
  0.0 82.7 jit_solution(6020227620751118648)
XLA Ops:
  0.6 0.0 copy-start
  0.6 0.9 %pad_maximum_fusion.kv_ref.w0 = bf16[256,256]{1,0:T(8,128)(2,1)S(1)} fusion(bf16[256,128]{1,0:T(8,128)(2,1)} %bitcast.12, bf16[256,128]{1,0:T(8,128)(2,1)} %bitcast.13), kind=kLoop, calls=%fused_computation | loop fusion | flops 262144 | bytes 262144 | tf_op jit(solution)/shard_map/concatenate | solution.py:334
  1.6 10.9 %collective-permute-start.3 = (bf16[256,256]{1,0:T(8,128)(2,1)S(1)}, bf16[256,256]{1,0:T(8,128)(2,1)S(1)}, u32[]{:S(2)}, u32[]{:S(2)}) collective-permute-start(bf16[256,256]{1,0:T(8,128)(2,1)S(1)} %pad_maximum_fusion.kv_ref.w0), channel_id=1, source_target_pairs={{0,8},{4,12},{8,16},{12,20},{16,24},{20,28},{24,32},{28,36},{32,40... | collective-permute-start | bytes 393224 | tf_op jit(solution)/shard_map/ppermute | solution.py:321
  12.5 1.9 %collective-permute-start.2 = (bf16[256,256]{1,0:T(8,128)(2,1)S(1)}, bf16[256,256]{1,0:T(8,128)(2,1)S(1)}, u32[]{:S(2)}, u32[]{:S(2)}) collective-permute-start(bf16[256,256]{1,0:T(8,128)(2,1)S(1)} %pad_maximum_fusion.kv_ref.w0), channel_id=1, source_target_pairs={{0,12},{4,16},{8,20},{12,24},{16,28},{20,32},{24,36},{28,40},{32,4... | collective-permute-start | bytes 393224 | tf_op jit(solution)/shard_map/ppermute | solution.py:321
  14.5 5.8 %collective-permute-start.1 = (bf16[256,256]{1,0:T(8,128)(2,1)S(1)}, bf16[256,256]{1,0:T(8,128)(2,1)S(1)}, u32[]{:S(2)}, u32[]{:S(2)}) collective-permute-start(bf16[256,256]{1,0:T(8,128)(2,1)S(1)} %pad_maximum_fusion.kv_ref.w0), channel_id=1, source_target_pairs={{0,4},{4,8},{8,12},{12,16},{16,20},{20,24},{24,28},{28,32},{32,36}... | collective-permute-start | bytes 393224 | tf_op jit(solution)/shard_map/ppermute | solution.py:321
  20.3 3.5 %collective-permute-start = (bf16[256,256]{1,0:T(8,128)(2,1)S(1)}, bf16[256,256]{1,0:T(8,128)(2,1)S(1)}, u32[]{:S(2)}, u32[]{:S(2)}) collective-permute-start(bf16[256,256]{1,0:T(8,128)(2,1)S(1)} %pad_maximum_fusion.kv_ref.w0), channel_id=1, source_target_pairs={{0,16},{4,20},{8,24},{12,28},{16,32},{20,36},{24,40},{28,44},{32,4... | collective-permute-start | bytes 393224 | tf_op jit(solution)/shard_map/ppermute | solution.py:321
  23.8 0.7 pad_maximum_fusion.1.gains_ref
  24.5 0.0 copy-start.1
  24.5 1.0 %copy-done.1 = bf16[1,256,1024]{2,1,0:T(8,128)(2,1)S(1)} copy-done((bf16[1,256,1024]{2,1,0:T(8,128)(2,1)S(1)}, bf16[1,256,1024]{2,1,0:T(8,128)(2,1)}, u32[]{:S(2)}) %copy-start.1) | copy-done | bytes 524312
  25.5 0.0 copy-start.2
  25.5 0.7 copy-done.2
  26.2 3.2 %prep.1 = (f32[1280,128]{1,0:T(8,128)S(1)}, f32[1280,128]{1,0:T(8,128)S(1)}, f32[1280,256]{1,0:T(8,128)S(1)}, bf16[8,256,128]{2,1,0:T(8,128)(2,1)S(1)}, f32[8,25...) custom-call(s32[1]{0:T(128)} %bitcast.first_ref, ...), custom_call_target="tpu_custom_call" | custom-call | tf_op jit(solution)/shard_map/prep/pallas_call | solution.py:266
  29.4 0.0 collective-permute-done.3.w2
  29.4 0.0 collective-permute-done.2.w3
  29.4 0.0 collective-permute-done.1.w1
  29.4 0.0 collective-permute-done.w4
  29.4 0.0 copy-done
  29.4 4.8 %attention.1 = (bf16[256,1024]{1,0:T(8,128)(2,1)}, f32[256,256]{1,0:T(8,128)S(1)}, bf16[256,256]{1,0:T(8,128)(2,1)S(1)}, bf16[256,256]{1,0:T(8,128)(2,1)S(1)}, b...) custom-call(s32[1]{0:T(128)} %get-tuple-element.23.scal_ref, ...), custom_call_target="tpu_custom_call" | custom-call | tf_op jit(solution)/shard_map/attention/pallas_call | solution.py:285
  34.2 11.5 %all-to-all-start = ((f32[64,2,128]{2,1,0:T(2,128)}), f32[64,2,128]{2,1,0:T(2,128)S(1)}, u32[]{:S(2)}, u32[]{:S(2)}) async-start(f32[64,2,128]{2,1,0:T(2,128)} %get-tuple-element.41), calls=%async_computation | async-start | bytes 131072 | tf_op jit(solution)/shard_map/all_to_all | solution.py:325
  45.7 12.0 %collective-permute-start.4 = (bf16[256,256]{1,0:T(8,128)(2,1)S(1)}, bf16[256,256]{1,0:T(8,128)(2,1)S(1)}, u32[]{:S(2)}, u32[]{:S(2)}) collective-permute-start(bf16[256,256]{1,0:T(8,128)(2,1)S(1)} %get-tuple-element.35), channel_id=1, source_target_pairs={{0,124},{4,0},{8,4},{12,8},{16,12},{20,16},{24,20},{28,24},{32,28}... | collective-permute-start | bytes 393224 | tf_op jit(solution)/shard_map/ppermute | solution.py:321
  57.7 4.3 %collective-permute-start.5 = (bf16[256,256]{1,0:T(8,128)(2,1)S(1)}, bf16[256,256]{1,0:T(8,128)(2,1)S(1)}, u32[]{:S(2)}, u32[]{:S(2)}) collective-permute-start(bf16[256,256]{1,0:T(8,128)(2,1)S(1)} %get-tuple-element.36), channel_id=1, source_target_pairs={{0,120},{4,124},{8,0},{12,4},{16,8},{20,12},{24,16},{28,20},{32,24... | collective-permute-start | bytes 393224 | tf_op jit(solution)/shard_map/ppermute | solution.py:321
  62.0 5.3 %collective-permute-start.6 = (bf16[256,256]{1,0:T(8,128)(2,1)S(1)}, bf16[256,256]{1,0:T(8,128)(2,1)S(1)}, u32[]{:S(2)}, u32[]{:S(2)}) collective-permute-start(bf16[256,256]{1,0:T(8,128)(2,1)S(1)} %get-tuple-element.37), channel_id=1, source_target_pairs={{0,116},{4,120},{8,124},{12,0},{16,4},{20,8},{24,12},{28,16},{32,2... | collective-permute-start | bytes 393224 | tf_op jit(solution)/shard_map/ppermute | solution.py:321
  67.2 3.3 %collective-permute-start.7 = (bf16[256,256]{1,0:T(8,128)(2,1)S(1)}, bf16[256,256]{1,0:T(8,128)(2,1)S(1)}, u32[]{:S(2)}, u32[]{:S(2)}) collective-permute-start(bf16[256,256]{1,0:T(8,128)(2,1)S(1)} %get-tuple-element.38), channel_id=1, source_target_pairs={{0,112},{4,116},{8,120},{12,124},{16,0},{20,4},{24,8},{28,12},{32,... | collective-permute-start | bytes 393224 | tf_op jit(solution)/shard_map/ppermute | solution.py:321
  70.5 0.0 all-to-all-done
  70.5 0.1 reduce_sum.18
  70.6 0.6 broadcast_in_dim.18
  71.2 3.3 %all-to-all-start.1 = ((f32[8,2,128]{2,1,0:T(2,128)}), f32[8,2,128]{2,1,0:T(2,128)S(1)}, u32[]{:S(2)}, u32[]{:S(2)}) async-start(f32[8,2,128]{2,1,0:T(2,128)} %broadcast_in_dim.18), calls=%async_computation.1 | async-start | bytes 16384 | tf_op jit(solution)/shard_map/all_to_all | solution.py:325
  74.5 0.0 collective-permute-done.4.r1
  74.5 0.8 collective-permute-done.5.r2
  75.3 0.0 collective-permute-done.6.r3
  75.3 0.0 collective-permute-done.7.r4
  75.3 0.9 %finish.1 = (bf16[256,128]{1,0:T(8,128)(2,1)}, bf16[256,128]{1,0:T(8,128)(2,1)}) custom-call(f32[256,256]{1,0:T(8,128)S(1)} %get-tuple-element.34.own_ref, bf16[256,256]{1,0:T(8,128)(2,1)S(1)} %collective-permute-done.4.r1, bf16[256,256]{1,0:T(8,128)(2,1)S(1)} %collective-permute-done.5.r2, bf16[256,256]{1,0:T(8,128)(2,1)S(1)} %collective-permute-done.6.r3, ...), custom_call_target="tpu_custom_call" | custom-call | tf_op jit(solution)/shard_map/finish/pallas_call | solution.py:305
  76.2 6.0 %all-to-all-done.1 = f32[8,2,128]{2,1,0:T(2,128)S(1)} async-done(((f32[8,2,128]{2,1,0:T(2,128)}), f32[8,2,128]{2,1,0:T(2,128)S(1)}, u32[]{:S(2)}, u32[]{:S(2)}) %all-to-all-start.1) | async-done | bytes 8224 | tf_op jit(solution)/shard_map/all_to_all | solution.py:325
  82.2 0.6 broadcast_multiply_fusion
  (1 shorter events, 0.0 us)
Async XLA Ops:
  0.6 28.8 %copy-start = (bf16[1,256,1024]{2,1,0:T(8,128)(2,1)S(1)}, bf16[1,256,1024]{2,1,0:T(8,128)(2,1)}, u32[]{:S(2)}) copy-start(bf16[1,256,1024]{2,1,0:T(8,128)(2,1)} %param.10) | copy-start | bytes 1572868
  1.6 27.8 %collective-permute-start.3 = (bf16[256,256]{1,0:T(8,128)(2,1)S(1)}, bf16[256,256]{1,0:T(8,128)(2,1)S(1)}, u32[]{:S(2)}, u32[]{:S(2)}) collective-permute-start(bf16[256,256]{1,0:T(8,128)(2,1)S(1)} %pad_maximum_fusion.kv_ref.w0), channel_id=1, source_target_pairs={{0,8},{4,12},{8,16},{12,20},{16,24},{20,28},{24,32},{28,36},{32,40... | collective-permute-start | bytes 393224 | tf_op jit(solution)/shard_map/ppermute | solution.py:321
  12.5 16.9 %collective-permute-start.2 = (bf16[256,256]{1,0:T(8,128)(2,1)S(1)}, bf16[256,256]{1,0:T(8,128)(2,1)S(1)}, u32[]{:S(2)}, u32[]{:S(2)}) collective-permute-start(bf16[256,256]{1,0:T(8,128)(2,1)S(1)} %pad_maximum_fusion.kv_ref.w0), channel_id=1, source_target_pairs={{0,12},{4,16},{8,20},{12,24},{16,28},{20,32},{24,36},{28,40},{32,4... | collective-permute-start | bytes 393224 | tf_op jit(solution)/shard_map/ppermute | solution.py:321
  14.5 15.0 %collective-permute-start.1 = (bf16[256,256]{1,0:T(8,128)(2,1)S(1)}, bf16[256,256]{1,0:T(8,128)(2,1)S(1)}, u32[]{:S(2)}, u32[]{:S(2)}) collective-permute-start(bf16[256,256]{1,0:T(8,128)(2,1)S(1)} %pad_maximum_fusion.kv_ref.w0), channel_id=1, source_target_pairs={{0,4},{4,8},{8,12},{12,16},{16,20},{20,24},{24,28},{28,32},{32,36}... | collective-permute-start | bytes 393224 | tf_op jit(solution)/shard_map/ppermute | solution.py:321
  20.3 9.1 %collective-permute-start = (bf16[256,256]{1,0:T(8,128)(2,1)S(1)}, bf16[256,256]{1,0:T(8,128)(2,1)S(1)}, u32[]{:S(2)}, u32[]{:S(2)}) collective-permute-start(bf16[256,256]{1,0:T(8,128)(2,1)S(1)} %pad_maximum_fusion.kv_ref.w0), channel_id=1, source_target_pairs={{0,16},{4,20},{8,24},{12,28},{16,32},{20,36},{24,40},{28,44},{32,4... | collective-permute-start | bytes 393224 | tf_op jit(solution)/shard_map/ppermute | solution.py:321
  24.5 1.0 %copy-start.1 = (bf16[1,256,1024]{2,1,0:T(8,128)(2,1)S(1)}, bf16[1,256,1024]{2,1,0:T(8,128)(2,1)}, u32[]{:S(2)}) copy-start(bf16[1,256,1024]{2,1,0:T(8,128)(2,1)} %param.7) | copy-start | bytes 1572868
  25.5 0.7 copy-start.2
  34.2 36.3 %all-to-all-start = ((f32[64,2,128]{2,1,0:T(2,128)}), f32[64,2,128]{2,1,0:T(2,128)S(1)}, u32[]{:S(2)}, u32[]{:S(2)}) async-start(f32[64,2,128]{2,1,0:T(2,128)} %get-tuple-element.41), calls=%async_computation | async-start | bytes 131072 | tf_op jit(solution)/shard_map/all_to_all | solution.py:325
  45.7 28.8 %collective-permute-start.4 = (bf16[256,256]{1,0:T(8,128)(2,1)S(1)}, bf16[256,256]{1,0:T(8,128)(2,1)S(1)}, u32[]{:S(2)}, u32[]{:S(2)}) collective-permute-start(bf16[256,256]{1,0:T(8,128)(2,1)S(1)} %get-tuple-element.35), channel_id=1, source_target_pairs={{0,124},{4,0},{8,4},{12,8},{16,12},{20,16},{24,20},{28,24},{32,28}... | collective-permute-start | bytes 393224 | tf_op jit(solution)/shard_map/ppermute | solution.py:321
  57.7 17.6 %collective-permute-start.5 = (bf16[256,256]{1,0:T(8,128)(2,1)S(1)}, bf16[256,256]{1,0:T(8,128)(2,1)S(1)}, u32[]{:S(2)}, u32[]{:S(2)}) collective-permute-start(bf16[256,256]{1,0:T(8,128)(2,1)S(1)} %get-tuple-element.36), channel_id=1, source_target_pairs={{0,120},{4,124},{8,0},{12,4},{16,8},{20,12},{24,16},{28,20},{32,24... | collective-permute-start | bytes 393224 | tf_op jit(solution)/shard_map/ppermute | solution.py:321
  62.0 13.3 %collective-permute-start.6 = (bf16[256,256]{1,0:T(8,128)(2,1)S(1)}, bf16[256,256]{1,0:T(8,128)(2,1)S(1)}, u32[]{:S(2)}, u32[]{:S(2)}) collective-permute-start(bf16[256,256]{1,0:T(8,128)(2,1)S(1)} %get-tuple-element.37), channel_id=1, source_target_pairs={{0,116},{4,120},{8,124},{12,0},{16,4},{20,8},{24,12},{28,16},{32,2... | collective-permute-start | bytes 393224 | tf_op jit(solution)/shard_map/ppermute | solution.py:321
  67.2 8.1 %collective-permute-start.7 = (bf16[256,256]{1,0:T(8,128)(2,1)S(1)}, bf16[256,256]{1,0:T(8,128)(2,1)S(1)}, u32[]{:S(2)}, u32[]{:S(2)}) collective-permute-start(bf16[256,256]{1,0:T(8,128)(2,1)S(1)} %get-tuple-element.38), channel_id=1, source_target_pairs={{0,112},{4,116},{8,120},{12,124},{16,0},{20,4},{24,8},{28,12},{32,... | collective-permute-start | bytes 393224 | tf_op jit(solution)/shard_map/ppermute | solution.py:321
  71.2 10.9 %all-to-all-start.1 = ((f32[8,2,128]{2,1,0:T(2,128)}), f32[8,2,128]{2,1,0:T(2,128)S(1)}, u32[]{:S(2)}, u32[]{:S(2)}) async-start(f32[8,2,128]{2,1,0:T(2,128)} %broadcast_in_dim.18), calls=%async_computation.1 | async-start | bytes 16384 | tf_op jit(solution)/shard_map/all_to_all | solution.py:325

commit v4 on v3

--- a/solution.py
+++ b/solution.py
@@ -53,13 +53,12 @@
 
 
 def prep_kernel(
-    rows, docs, first_ref, lens_ref, gains_ref, q_ref, kv_ref,
+    rows, first_ref, packed_ref, q_ref, kv_ref,
     cos_ref, sin_ref, bias_ref, qrot_ref, qnorm_ref, qinv_ref, krot_ref, knorm_ref, gain_ref, scal_ref,
 ):
     first = first_ref[0]
     chunks = rows // CHUNK
     heads = q_ref.shape[1] // HD
-    tok_row = lax.broadcasted_iota(jnp.int32, (8, rows), 1)
     lane = lax.broadcasted_iota(jnp.int32, (8, HD), 1)
     row8 = lax.broadcasted_iota(jnp.int32, (8, HD), 0)
     sign = jnp.where(lane[0:1] < HALF, -1.0, 1.0).astype(jnp.float32)
@@ -68,20 +67,18 @@
     within = lax.broadcasted_iota(jnp.int32, (CHUNK, HD), 0).astype(jnp.float32) * freq
     within_c, within_s = jnp.cos(within), jnp.sin(within)
 
-    def one_doc(d, carry):
-        start, reaching, row = carry
-        rel = start - first
-        start = start + lens_ref[0, d]
-        reaching = jnp.where(rel <= 0, rel, reaching)
-        row = jnp.where(tok_row >= rel, rel, row)
-        return start, reaching, row
-
-    zero = jnp.int32(0)
-    _, reaching, low = lax.fori_loop(0, docs, one_doc, (zero, zero, jnp.zeros((8, rows), jnp.int32)))
-    before = -reaching
-    scal_ref[0] = 1 + (before + rows - 1) // rows
-    position = (tok_row - low).astype(jnp.float32)
-    columns = [jnp.broadcast_to(position[0:1, chunk_rows(c)], (CHUNK, CHUNK)).T for c in range(chunks)]
+    inner = lax.broadcasted_iota(jnp.int32, (HD, HD), 1) < lax.broadcasted_iota(jnp.int32, (HD, HD), 0)
+    starts = jnp.sum(jnp.where(inner, packed_ref[2:3], 0.0), axis=1, keepdims=True)
+    rel = starts - first.astype(jnp.float32)
+    tok = lax.broadcasted_iota(jnp.int32, (HD, rows), 1).astype(jnp.float32)
+    low = jnp.max(jnp.where(rel <= tok, rel, MASKED), axis=0, keepdims=True)
+    before = -jnp.max(jnp.where(rel <= 0.0, rel, MASKED))
+    count = jnp.int32(1)
+    for d in range(REACH):
+        count = count + jnp.where(before > float(d * rows), 1, 0)
+    scal_ref[0] = count
+    position = tok[0:1] - low
+    columns = [jnp.broadcast_to(position[:, chunk_rows(c)], (CHUNK, CHUNK)).T for c in range(chunks)]
     angles = jnp.where(lane[0:1] < HALF, columns[0], columns[1]) * freq
     packed_c, packed_s = jnp.cos(angles), jnp.sin(angles)
     rolled_c, rolled_s = pltpu.roll(packed_c, HALF, 1), pltpu.roll(packed_s, HALF, 1)
@@ -91,7 +88,7 @@
     sin = sin * sign
     cos_ref[0:rows, :] = cos
     sin_ref[0:rows, :] = sin
-    base = (before - rows * (row8 // chunks + 1) + CHUNK * (row8 % chunks)).astype(jnp.float32) * freq
+    base = (before + (CHUNK * (row8 % chunks) - rows * (row8 // chunks + 1)).astype(jnp.float32)) * freq
     base_c, base_s = jnp.cos(base), jnp.sin(base)
     for j in range(chunks * REACH):
         at = chunk_rows(chunks + j)
@@ -100,14 +97,15 @@
         sin_ref[at, :] = (s * within_c + c * within_s) * sign
     key = lax.broadcasted_iota(jnp.int32, (CHUNK, rows), 0)
     tok = lax.broadcasted_iota(jnp.int32, (CHUNK, rows), 1)
+    low = low.astype(jnp.int32)
     for i in range(chunks + chunks * REACH):
         offset = i % chunks * CHUNK - i // chunks * rows
-        kept = key + offset >= low[0:1, :]
+        kept = key + offset >= low
         if i < chunks:
             kept = kept & (key + offset <= tok)
         bias_ref[chunk_rows(i), :] = jnp.where(kept, 0.0, MASKED)
-    gain_ref[...] = gains_ref[...]
-    q_gain, k_gain = gains_ref[0:1], gains_ref[1:2]
+    gain_ref[...] = packed_ref[0:2]
+    q_gain, k_gain = packed_ref[0:1], packed_ref[1:2]
     normed, _ = normed_of(kv_ref[:, :HD])
     knorm_ref[...] = normed
     krot_ref[...] = rope(normed * k_gain, cos, sin).astype(jnp.bfloat16)
@@ -258,14 +256,13 @@
     return pltpu.CompilerParams(vmem_limit_bytes=mib * 1024 * 1024)
 
 
-def prepare(doc_lengths, first, gains, queries, kv):
-    docs = doc_lengths.shape[1]
+def prepare(first, packed, queries, kv):
     rows, width = queries.shape
     heads = width // HD
     size = BLOCKS * rows
     return pl.pallas_call(
-        functools.partial(prep_kernel, rows, docs),
-        in_specs=[SMEM, SMEM] + [VMEM] * 3,
+        functools.partial(prep_kernel, rows),
+        in_specs=[SMEM] + [VMEM] * 3,
         out_specs=[VMEM] * 9 + [SMEM],
         out_shape=[
             F32((size, HD)), F32((size, HD)), F32((size, rows)),
@@ -275,7 +272,7 @@
         ],
         compiler_params=limit(24),
         name="prep",
-    )(first, doc_lengths, gains, queries, kv)
+    )(first, packed, queries, kv)
 
 
 def attention(prepared, grads, window, fan):
@@ -334,7 +331,8 @@
     kv = jnp.concatenate([keys_raw[0], values[0]], axis=1)
     got = {d: shifted(kv, d) for d in (2, 3, 1, 4)}
     first = (shard * rows).astype(jnp.int32).reshape(1)
-    prepared = prepare(doc_lengths, first, jnp.stack([q_gain, k_gain]), queries_raw[0], kv)
+    lengths = jnp.pad(doc_lengths[0].astype(jnp.float32), (0, HD - doc_lengths.shape[1]))
+    prepared = prepare(first, jnp.stack([q_gain, k_gain, lengths]), queries_raw[0], kv)
     window = [kv] + [got[d] for d in range(1, BLOCKS)]
     dq, own, *terms, gains = attention(prepared, grad_out[0], window, fan)
     back = {d: shifted(terms[d - 1], -d) for d in (2, 3, 1, 4)}

time: 83.2 us -> 84.2 us (1.012); the launches traced: 82.7 us -> 82.7 us
  Pallas kernels: 8.87 us -> 7.69 us
  starting transfers between devices: 61.7 us -> 62.7 us
    all_to_all x2, starting transfers between devices: 14.7 us -> 18.5 us  [exchanged(): return jnp.sum(lax.all_to_all(copies, axes, 0, 0), axis=0)]
    ppermute x8, starting transfers between devices: 46.9 us -> 44.2 us  [shifted(): lax.ppermute(block, CTX, [(i, (i + distance) % count) for i in range(coun...]
    pallas_call x1, Pallas kernels: 3.22 us -> 2.04 us  [prepare(): pl.pallas_call(functools.partial(prep_kernel, rows), in_specs=[SMEM] + [V...]
    unnamed x6 -> x4, local copies, waits for them, and re-layouts: 1.7 us -> 1.04 us
  transfers between devices with their start and end apart: 10 -> 10, of which waited for: 2 -> 3; matrix products, arithmetic and copies ran while one was open for 2% -> 2% of each run, Pallas kernels for 5% -> 4%
where the time goes in v4:
time: 84.2 us; the launch traced here: 82.7 us
  starting transfers between devices  62.7 us (74%)
  Pallas kernels  7.69 us (9%)
  waiting for transfers between devices  6.96 us (8%)
  other arithmetic  2.95 us (4%)
  local copies, waits for them, and re-layouts  1.65 us (2%)
    ppermute x8, starting transfers between devices, shifted(): lax.ppermute(block, CTX, [(i, (i + distance) % count) for i in range(coun...  44.2 us
    all_to_all x2, starting transfers between devices, exchanged(): return jnp.sum(lax.all_to_all(copies, axes, 0, 0), axis=0)  18.5 us
    all_to_all x2, waiting for transfers between devices, exchanged(): return jnp.sum(lax.all_to_all(copies, axes, 0, 0), axis=0)  6.39 us
    pallas_call x1, Pallas kernels, attention(): pl.pallas_call(functools.partial(main_kernel, rows), in_specs=[SMEM] + [V...  4.79 us
    pallas_call x1, Pallas kernels, prepare(): pl.pallas_call(functools.partial(prep_kernel, rows), in_specs=[SMEM] + [V...  2.04 us
  transfers between devices with their start and end apart: 10, of which 3 were waited for; matrix products, arithmetic and copies ran while one was open for 2% of the time, Pallas kernels for 4%

profile of v4, /device:TPU:2, one launch (start us, length us, event | category | flops | bytes accessed | tf_op | source)
XLA Modules:
  0.0 82.7 jit_solution(18358180718781603105)
XLA Ops:
  0.6 0.0 copy-start
  0.6 0.9 %pad_maximum_fusion.kv_ref.w0 = bf16[256,256]{1,0:T(8,128)(2,1)S(1)} fusion(bf16[256,128]{1,0:T(8,128)(2,1)} %bitcast.16, bf16[256,128]{1,0:T(8,128)(2,1)} %bitcast.17), kind=kLoop, calls=%fused_computation | loop fusion | flops 262144 | bytes 262144 | tf_op jit(solution)/shard_map/concatenate | solution.py:331
  1.6 10.9 %collective-permute-start.3 = (bf16[256,256]{1,0:T(8,128)(2,1)S(1)}, bf16[256,256]{1,0:T(8,128)(2,1)S(1)}, u32[]{:S(2)}, u32[]{:S(2)}) collective-permute-start(bf16[256,256]{1,0:T(8,128)(2,1)S(1)} %pad_maximum_fusion.kv_ref.w0), channel_id=1, source_target_pairs={{0,8},{4,12},{8,16},{12,20},{16,24},{20,28},{24,32},{28,36},{32,40... | collective-permute-start | bytes 393224 | tf_op jit(solution)/shard_map/ppermute | solution.py:318
  12.5 1.9 %collective-permute-start.2 = (bf16[256,256]{1,0:T(8,128)(2,1)S(1)}, bf16[256,256]{1,0:T(8,128)(2,1)S(1)}, u32[]{:S(2)}, u32[]{:S(2)}) collective-permute-start(bf16[256,256]{1,0:T(8,128)(2,1)S(1)} %pad_maximum_fusion.kv_ref.w0), channel_id=1, source_target_pairs={{0,12},{4,16},{8,20},{12,24},{16,28},{20,32},{24,36},{28,40},{32,4... | collective-permute-start | bytes 393224 | tf_op jit(solution)/shard_map/ppermute | solution.py:318
  14.5 5.8 %collective-permute-start.1 = (bf16[256,256]{1,0:T(8,128)(2,1)S(1)}, bf16[256,256]{1,0:T(8,128)(2,1)S(1)}, u32[]{:S(2)}, u32[]{:S(2)}) collective-permute-start(bf16[256,256]{1,0:T(8,128)(2,1)S(1)} %pad_maximum_fusion.kv_ref.w0), channel_id=1, source_target_pairs={{0,4},{4,8},{8,12},{12,16},{16,20},{20,24},{24,28},{28,32},{32,36}... | collective-permute-start | bytes 393224 | tf_op jit(solution)/shard_map/ppermute | solution.py:318
  20.3 3.5 %collective-permute-start = (bf16[256,256]{1,0:T(8,128)(2,1)S(1)}, bf16[256,256]{1,0:T(8,128)(2,1)S(1)}, u32[]{:S(2)}, u32[]{:S(2)}) collective-permute-start(bf16[256,256]{1,0:T(8,128)(2,1)S(1)} %pad_maximum_fusion.kv_ref.w0), channel_id=1, source_target_pairs={{0,16},{4,20},{8,24},{12,28},{16,32},{20,36},{24,40},{28,44},{32,4... | collective-permute-start | bytes 393224 | tf_op jit(solution)/shard_map/ppermute | solution.py:318
  23.8 0.7 convert_bitcast_fusion
  24.4 0.7 pad_maximum_fusion.1.packed_ref
  25.1 0.0 copy-start.1
  25.1 1.0 %copy-done.1 = bf16[1,256,1024]{2,1,0:T(8,128)(2,1)S(1)} copy-done((bf16[1,256,1024]{2,1,0:T(8,128)(2,1)S(1)}, bf16[1,256,1024]{2,1,0:T(8,128)(2,1)}, u32[]{:S(2)}) %copy-start.1) | copy-done | bytes 524312
  26.2 2.0 %prep.1 = (f32[1280,128]{1,0:T(8,128)S(1)}, f32[1280,128]{1,0:T(8,128)S(1)}, f32[1280,256]{1,0:T(8,128)S(1)}, bf16[8,256,128]{2,1,0:T(8,128)(2,1)S(1)}, f32[8,25...) custom-call(s32[1]{0:T(128)} %bitcast.first_ref, ...), custom_call_target="tpu_custom_call" | custom-call | tf_op jit(solution)/shard_map/prep/pallas_call | solution.py:263
  28.2 0.0 collective-permute-done.3.w2
  28.2 0.0 collective-permute-done.2.w3
  28.2 0.0 collective-permute-done.1.w1
  28.2 0.1 collective-permute-done.w4
  28.4 0.0 copy-done
  28.4 4.8 %attention.1 = (bf16[256,1024]{1,0:T(8,128)(2,1)}, f32[256,256]{1,0:T(8,128)S(1)}, bf16[256,256]{1,0:T(8,128)(2,1)S(1)}, bf16[256,256]{1,0:T(8,128)(2,1)S(1)}, b...) custom-call(s32[1]{0:T(128)} %get-tuple-element.23.scal_ref, ...), custom_call_target="tpu_custom_call" | custom-call | tf_op jit(solution)/shard_map/attention/pallas_call | solution.py:282
  33.1 14.7 %all-to-all-start = ((f32[64,2,128]{2,1,0:T(2,128)}), f32[64,2,128]{2,1,0:T(2,128)S(1)}, u32[]{:S(2)}, u32[]{:S(2)}) async-start(f32[64,2,128]{2,1,0:T(2,128)} %get-tuple-element.41), calls=%async_computation | async-start | bytes 131072 | tf_op jit(solution)/shard_map/all_to_all | solution.py:322
  47.9 6.1 %collective-permute-start.4 = (bf16[256,256]{1,0:T(8,128)(2,1)S(1)}, bf16[256,256]{1,0:T(8,128)(2,1)S(1)}, u32[]{:S(2)}, u32[]{:S(2)}) collective-permute-start(bf16[256,256]{1,0:T(8,128)(2,1)S(1)} %get-tuple-element.35), channel_id=1, source_target_pairs={{0,124},{4,0},{8,4},{12,8},{16,12},{20,16},{24,20},{28,24},{32,28}... | collective-permute-start | bytes 393224 | tf_op jit(solution)/shard_map/ppermute | solution.py:318
  54.0 4.3 %collective-permute-start.5 = (bf16[256,256]{1,0:T(8,128)(2,1)S(1)}, bf16[256,256]{1,0:T(8,128)(2,1)S(1)}, u32[]{:S(2)}, u32[]{:S(2)}) collective-permute-start(bf16[256,256]{1,0:T(8,128)(2,1)S(1)} %get-tuple-element.36), channel_id=1, source_target_pairs={{0,120},{4,124},{8,0},{12,4},{16,8},{20,12},{24,16},{28,20},{32,24... | collective-permute-start | bytes 393224 | tf_op jit(solution)/shard_map/ppermute | solution.py:318
  58.2 9.7 %collective-permute-start.6 = (bf16[256,256]{1,0:T(8,128)(2,1)S(1)}, bf16[256,256]{1,0:T(8,128)(2,1)S(1)}, u32[]{:S(2)}, u32[]{:S(2)}) collective-permute-start(bf16[256,256]{1,0:T(8,128)(2,1)S(1)} %get-tuple-element.37), channel_id=1, source_target_pairs={{0,116},{4,120},{8,124},{12,0},{16,4},{20,8},{24,12},{28,16},{32,2... | collective-permute-start | bytes 393224 | tf_op jit(solution)/shard_map/ppermute | solution.py:318
  68.0 1.9 %collective-permute-start.7 = (bf16[256,256]{1,0:T(8,128)(2,1)S(1)}, bf16[256,256]{1,0:T(8,128)(2,1)S(1)}, u32[]{:S(2)}, u32[]{:S(2)}) collective-permute-start(bf16[256,256]{1,0:T(8,128)(2,1)S(1)} %get-tuple-element.38), channel_id=1, source_target_pairs={{0,112},{4,116},{8,120},{12,124},{16,0},{20,4},{24,8},{28,12},{32,... | collective-permute-start | bytes 393224 | tf_op jit(solution)/shard_map/ppermute | solution.py:318
  69.9 0.0 all-to-all-done
  69.9 0.1 reduce_sum.18
  70.0 0.6 broadcast_in_dim.18
  70.6 3.8 %all-to-all-start.1 = ((f32[8,2,128]{2,1,0:T(2,128)}), f32[8,2,128]{2,1,0:T(2,128)S(1)}, u32[]{:S(2)}, u32[]{:S(2)}) async-start(f32[8,2,128]{2,1,0:T(2,128)} %broadcast_in_dim.18), calls=%async_computation.1 | async-start | bytes 16384 | tf_op jit(solution)/shard_map/all_to_all | solution.py:322
  74.4 0.0 collective-permute-done.4.r1
  74.4 0.0 collective-permute-done.5.r2
  74.4 0.0 collective-permute-done.6.r3
  74.4 0.4 collective-permute-done.7.r4
  74.8 0.9 %finish.1 = (bf16[256,128]{1,0:T(8,128)(2,1)}, bf16[256,128]{1,0:T(8,128)(2,1)}) custom-call(f32[256,256]{1,0:T(8,128)S(1)} %get-tuple-element.34.own_ref, bf16[256,256]{1,0:T(8,128)(2,1)S(1)} %collective-permute-done.4.r1, bf16[256,256]{1,0:T(8,128)(2,1)S(1)} %collective-permute-done.5.r2, bf16[256,256]{1,0:T(8,128)(2,1)S(1)} %collective-permute-done.6.r3, ...), custom_call_target="tpu_custom_call" | custom-call | tf_op jit(solution)/shard_map/finish/pallas_call | solution.py:302
  75.7 6.4 %all-to-all-done.1 = f32[8,2,128]{2,1,0:T(2,128)S(1)} async-done(((f32[8,2,128]{2,1,0:T(2,128)}), f32[8,2,128]{2,1,0:T(2,128)S(1)}, u32[]{:S(2)}, u32[]{:S(2)}) %all-to-all-start.1) | async-done | bytes 8224 | tf_op jit(solution)/shard_map/all_to_all | solution.py:322
  82.1 0.6 broadcast_multiply_fusion
  (2 shorter events, 0.0 us)
Async XLA Ops:
  0.6 27.7 %copy-start = (bf16[1,256,1024]{2,1,0:T(8,128)(2,1)S(1)}, bf16[1,256,1024]{2,1,0:T(8,128)(2,1)}, u32[]{:S(2)}) copy-start(bf16[1,256,1024]{2,1,0:T(8,128)(2,1)} %param.10) | copy-start | bytes 1572868
  1.6 26.6 %collective-permute-start.3 = (bf16[256,256]{1,0:T(8,128)(2,1)S(1)}, bf16[256,256]{1,0:T(8,128)(2,1)S(1)}, u32[]{:S(2)}, u32[]{:S(2)}) collective-permute-start(bf16[256,256]{1,0:T(8,128)(2,1)S(1)} %pad_maximum_fusion.kv_ref.w0), channel_id=1, source_target_pairs={{0,8},{4,12},{8,16},{12,20},{16,24},{20,28},{24,32},{28,36},{32,40... | collective-permute-start | bytes 393224 | tf_op jit(solution)/shard_map/ppermute | solution.py:318
  12.5 15.7 %collective-permute-start.2 = (bf16[256,256]{1,0:T(8,128)(2,1)S(1)}, bf16[256,256]{1,0:T(8,128)(2,1)S(1)}, u32[]{:S(2)}, u32[]{:S(2)}) collective-permute-start(bf16[256,256]{1,0:T(8,128)(2,1)S(1)} %pad_maximum_fusion.kv_ref.w0), channel_id=1, source_target_pairs={{0,12},{4,16},{8,20},{12,24},{16,28},{20,32},{24,36},{28,40},{32,4... | collective-permute-start | bytes 393224 | tf_op jit(solution)/shard_map/ppermute | solution.py:318
  14.5 13.8 %collective-permute-start.1 = (bf16[256,256]{1,0:T(8,128)(2,1)S(1)}, bf16[256,256]{1,0:T(8,128)(2,1)S(1)}, u32[]{:S(2)}, u32[]{:S(2)}) collective-permute-start(bf16[256,256]{1,0:T(8,128)(2,1)S(1)} %pad_maximum_fusion.kv_ref.w0), channel_id=1, source_target_pairs={{0,4},{4,8},{8,12},{12,16},{16,20},{20,24},{24,28},{28,32},{32,36}... | collective-permute-start | bytes 393224 | tf_op jit(solution)/shard_map/ppermute | solution.py:318
  20.3 8.1 %collective-permute-start = (bf16[256,256]{1,0:T(8,128)(2,1)S(1)}, bf16[256,256]{1,0:T(8,128)(2,1)S(1)}, u32[]{:S(2)}, u32[]{:S(2)}) collective-permute-start(bf16[256,256]{1,0:T(8,128)(2,1)S(1)} %pad_maximum_fusion.kv_ref.w0), channel_id=1, source_target_pairs={{0,16},{4,20},{8,24},{12,28},{16,32},{20,36},{24,40},{28,44},{32,4... | collective-permute-start | bytes 393224 | tf_op jit(solution)/shard_map/ppermute | solution.py:318
  25.1 1.0 %copy-start.1 = (bf16[1,256,1024]{2,1,0:T(8,128)(2,1)S(1)}, bf16[1,256,1024]{2,1,0:T(8,128)(2,1)}, u32[]{:S(2)}) copy-start(bf16[1,256,1024]{2,1,0:T(8,128)(2,1)} %param.7) | copy-start | bytes 1572868
  33.1 36.8 %all-to-all-start = ((f32[64,2,128]{2,1,0:T(2,128)}), f32[64,2,128]{2,1,0:T(2,128)S(1)}, u32[]{:S(2)}, u32[]{:S(2)}) async-start(f32[64,2,128]{2,1,0:T(2,128)} %get-tuple-element.41), calls=%async_computation | async-start | bytes 131072 | tf_op jit(solution)/shard_map/all_to_all | solution.py:322
  47.9 26.5 %collective-permute-start.4 = (bf16[256,256]{1,0:T(8,128)(2,1)S(1)}, bf16[256,256]{1,0:T(8,128)(2,1)S(1)}, u32[]{:S(2)}, u32[]{:S(2)}) collective-permute-start(bf16[256,256]{1,0:T(8,128)(2,1)S(1)} %get-tuple-element.35), channel_id=1, source_target_pairs={{0,124},{4,0},{8,4},{12,8},{16,12},{20,16},{24,20},{28,24},{32,28}... | collective-permute-start | bytes 393224 | tf_op jit(solution)/shard_map/ppermute | solution.py:318
  54.0 20.4 %collective-permute-start.5 = (bf16[256,256]{1,0:T(8,128)(2,1)S(1)}, bf16[256,256]{1,0:T(8,128)(2,1)S(1)}, u32[]{:S(2)}, u32[]{:S(2)}) collective-permute-start(bf16[256,256]{1,0:T(8,128)(2,1)S(1)} %get-tuple-element.36), channel_id=1, source_target_pairs={{0,120},{4,124},{8,0},{12,4},{16,8},{20,12},{24,16},{28,20},{32,24... | collective-permute-start | bytes 393224 | tf_op jit(solution)/shard_map/ppermute | solution.py:318
  58.2 16.2 %collective-permute-start.6 = (bf16[256,256]{1,0:T(8,128)(2,1)S(1)}, bf16[256,256]{1,0:T(8,128)(2,1)S(1)}, u32[]{:S(2)}, u32[]{:S(2)}) collective-permute-start(bf16[256,256]{1,0:T(8,128)(2,1)S(1)} %get-tuple-element.37), channel_id=1, source_target_pairs={{0,116},{4,120},{8,124},{12,0},{16,4},{20,8},{24,12},{28,16},{32,2... | collective-permute-start | bytes 393224 | tf_op jit(solution)/shard_map/ppermute | solution.py:318
  68.0 6.9 %collective-permute-start.7 = (bf16[256,256]{1,0:T(8,128)(2,1)S(1)}, bf16[256,256]{1,0:T(8,128)(2,1)S(1)}, u32[]{:S(2)}, u32[]{:S(2)}) collective-permute-start(bf16[256,256]{1,0:T(8,128)(2,1)S(1)} %get-tuple-element.38), channel_id=1, source_target_pairs={{0,112},{4,116},{8,120},{12,124},{16,0},{20,4},{24,8},{28,12},{32,... | collective-permute-start | bytes 393224 | tf_op jit(solution)/shard_map/ppermute | solution.py:318
  70.6 11.5 %all-to-all-start.1 = ((f32[8,2,128]{2,1,0:T(2,128)}), f32[8,2,128]{2,1,0:T(2,128)S(1)}, u32[]{:S(2)}, u32[]{:S(2)}) async-start(f32[8,2,128]{2,1,0:T(2,128)} %broadcast_in_dim.18), calls=%async_computation.1 | async-start | bytes 16384 | tf_op jit(solution)/shard_map/all_to_all | solution.py:322
